TPU v7x, 32 devices: a whole 2x2x4 slice. The times are simulated.
32 devices in a mesh: dp: 4 (over y, core), frame: 2 (over x), tensor: 4 (over z).
Axes of the slice: x: 2, y: 2, z: 4, core: 2. Of those that a mesh axis runs over, the one named last changes fastest.
Arguments:
- latent: bfloat16 [12, 16, 32, 128], P('dp', 'frame', 'tensor'), may hold values from -5 to 5
- noise_draw: bfloat16 [12, 16, 32, 128], P('dp', 'frame', 'tensor'), may hold values from -5 to 5
- levels: int32 [12, 16], P('dp', 'frame'), may hold values from 1 to 999
- context: int32 [12], replicated, may hold values from 1 to 15
- step_count: int32 [1], replicated, may hold values from 1 to 20
- w_in: float32 [1024, 7168], P(('dp', 'frame'), 'tensor'), may hold values from -0.1875 to 0.1875
- w_outs: float32 [5120, 1024], P('tensor', ('dp', 'frame')), may hold values from -2 to 2, as said below
- w_cond: float32 [1024, 8192], P(('dp', 'frame'), 'tensor'), may hold values from -0.1875 to 0.1875
- w_time: float32 [1280, 1024], P(('dp', 'frame')), may hold values from -0.5 to 0.5
- w_patch: float32 [2, 16, 1024], P(None, None, ('dp', 'frame')), may hold values from -0.75 to 0.75
- m_in: float32 [1024, 7168], P(('dp', 'frame'), 'tensor'), may hold values from -0.00012207031 to 0.00012207031
- m_outs: float32 [5120, 1024], P('tensor', ('dp', 'frame')), may hold values from -3.8146973e-05 to 3.8146973e-05
- m_cond: float32 [1024, 8192], P(('dp', 'frame'), 'tensor'), may hold values from -0.00012207031 to 0.00012207031
- m_time: float32 [1280, 1024], P(('dp', 'frame')), may hold values from -0.00012207031 to 0.00012207031
- m_patch: float32 [2, 16, 1024], P(None, None, ('dp', 'frame')), may hold values from -0.00012207031 to 0.00012207031
- v_in: float32 [1024, 7168], P(('dp', 'frame'), 'tensor'), may hold values from 4.481289e-10 to 1.7925156e-09
- v_outs: float32 [5120, 1024], P('tensor', ('dp', 'frame')), may hold values from 4.481289e-11 to 1.7925156e-10
- v_cond: float32 [1024, 8192], P(('dp', 'frame'), 'tensor'), may hold values from 4.481289e-10 to 1.7925156e-09
- v_time: float32 [1280, 1024], P(('dp', 'frame')), may hold values from 4.481289e-10 to 1.7925156e-09
- v_patch: float32 [2, 16, 1024], P(None, None, ('dp', 'frame')), may hold values from 4.481289e-10 to 1.7925156e-09
Outputs:
- loss_value: float32 [], replicated
- grad_norm: float32 [], replicated
- new_in: float32 [1024, 7168], P(('dp', 'frame'), 'tensor')
- new_outs: float32 [5120, 1024], P('tensor', ('dp', 'frame'))
- new_cond: float32 [1024, 8192], P(('dp', 'frame'), 'tensor')
- new_time: float32 [1280, 1024], P(('dp', 'frame'))
- new_patch: float32 [2, 16, 1024], P(None, None, ('dp', 'frame'))
- first_in: float32 [1024, 7168], P(('dp', 'frame'), 'tensor')
- first_outs: float32 [5120, 1024], P('tensor', ('dp', 'frame'))
- first_cond: float32 [1024, 8192], P(('dp', 'frame'), 'tensor')
- first_time: float32 [1280, 1024], P(('dp', 'frame'))
- first_patch: float32 [2, 16, 1024], P(None, None, ('dp', 'frame'))
- second_in: float32 [1024, 7168], P(('dp', 'frame'), 'tensor')
- second_outs: float32 [5120, 1024], P('tensor', ('dp', 'frame'))
- second_cond: float32 [1024, 8192], P(('dp', 'frame'), 'tensor')
- second_time: float32 [1280, 1024], P(('dp', 'frame'))
- second_patch: float32 [2, 16, 1024], P(None, None, ('dp', 'frame'))
- half_in: bfloat16 [1024, 7168], P(('dp', 'frame'), 'tensor')
- half_outs: bfloat16 [5120, 1024], P('tensor', ('dp', 'frame'))
- half_cond: bfloat16 [1024, 8192], P(('dp', 'frame'), 'tensor')
- half_time: bfloat16 [1280, 1024], P(('dp', 'frame'))
- half_patch: bfloat16 [2, 16, 1024], P(None, None, ('dp', 'frame'))
Inputs may be any that keep to these rules, and one draw needn't show every extreme that they name: `w_outs`: output-projection and down-projection weights.
All inputs are finite; a program needn't handle non-finite values.
Results may differ from a plain program's by a relative error of at most 0.017.
Values may be sent and summed in bfloat16 or wider, within the bound.
A program may use at most 512 MiB of HBM per device.

v0:
```python
from functools import partial
import math

import jax
import jax.numpy as jnp
from jax import lax
from jax.sharding import PartitionSpec as P

D = 1024
HD = 64
TEMB = 256
CHANNELS = 4
PATCH = 2
PD = 16
TOKF = 256
FRAMES = 16
NLEV = 1000
CLIP_DEV = 1
MB = 3


EPS_NORM = 1e-06
MAX_NORM = 0.1
LEARN_RATE = 0.08
WEIGHT_DECAY = 0.1
BETA_FIRST = 0.5
BETA_SECOND = 0.5
ADAM_EPS = 1e-08


def to_half(array_in):
    return array_in.astype(jnp.bfloat16)


def product(left_mat, right_mat):
    return jnp.dot(left_mat, right_mat, preferred_element_type=jnp.float32)


def rows_product(left_mat, right_mat):
    return lax.dot_general(
        left_mat, right_mat, (((0,), (0,)), ((), ())), preferred_element_type=jnp.float32
    )


def cols_product(left_mat, right_mat):
    return lax.dot_general(
        left_mat, right_mat, (((1,), (1,)), ((), ())), preferred_element_type=jnp.float32
    )


def frequency_table(level_values):
    half_width = TEMB // 2
    rate_table = jnp.exp(
        -math.log(10000.0) * jnp.arange(half_width, dtype=jnp.float32) / half_width
    )
    angles = level_values[..., None] * rate_table
    return jnp.concatenate([jnp.cos(angles), jnp.sin(angles)], axis=-1)


def noise_terms(level_values):
    angles = level_values * (0.5 * math.pi / NLEV)
    return (jnp.cos(angles), jnp.sin(angles))


def modulate(residual, shift_rows, scale_rows):
    centre = residual - jnp.mean(residual, axis=-1, keepdims=True)
    spread = jnp.mean(centre * centre, axis=-1, keepdims=True)
    return centre * lax.rsqrt(spread + EPS_NORM) * (1.0 + scale_rows) + shift_rows


def modulate_back(residual, shift_rows, scale_rows, grad_out):
    unused, pullback = jax.vjp(modulate, residual, shift_rows, scale_rows)
    return pullback(grad_out)


def patchify(field_in):
    lead_shape = field_in.shape[:-2]
    rows_here = field_in.shape[-2]
    width_cells = field_in.shape[-1] // CHANNELS
    lead_rank = len(lead_shape)
    blocks_view = field_in.reshape(
        lead_shape + (rows_here // PATCH, PATCH, width_cells // PATCH, PATCH, CHANNELS)
    )
    order_axes = tuple(range(lead_rank)) + (
        lead_rank,
        lead_rank + 2,
        lead_rank + 1,
        lead_rank + 3,
        lead_rank + 4,
    )
    return jnp.transpose(blocks_view, order_axes).reshape(
        lead_shape + (rows_here // PATCH * (width_cells // PATCH), PATCH * PATCH * CHANNELS)
    )


def gather_rows(array_in):
    return lax.all_gather(array_in, "tensor", axis=1, tiled=True)


def scatter_rows(array_in):
    return lax.psum_scatter(
        array_in.astype(jnp.bfloat16), "tensor", scatter_dimension=1, tiled=True
    ).astype(jnp.float32)


def fetch_weights(half_in, half_outs, half_cond, half_time, half_patch):
    return (
        lax.all_gather(half_in, ("dp", "frame"), axis=0, tiled=True),
        lax.all_gather(half_outs, ("dp", "frame"), axis=1, tiled=True),
        lax.all_gather(half_cond, ("dp", "frame"), axis=0, tiled=True),
        lax.all_gather(half_time, ("dp", "frame"), axis=0, tiled=True),
        lax.all_gather(half_patch, ("dp", "frame"), axis=2, tiled=True),
    )


def reduce_grads(grad_set):
    return (
        lax.psum_scatter(
            grad_set[0].astype(jnp.bfloat16), ("dp", "frame"), scatter_dimension=0, tiled=True
        ).astype(jnp.float32),
        lax.psum_scatter(
            grad_set[1].astype(jnp.bfloat16), ("dp", "frame"), scatter_dimension=1, tiled=True
        ).astype(jnp.float32),
        lax.psum_scatter(
            grad_set[2].astype(jnp.bfloat16), ("dp", "frame"), scatter_dimension=0, tiled=True
        ).astype(jnp.float32),
        lax.psum_scatter(
            grad_set[3].astype(jnp.bfloat16), ("dp", "frame"), scatter_dimension=0, tiled=True
        ).astype(jnp.float32),
        lax.psum_scatter(
            grad_set[4].astype(jnp.bfloat16), ("dp", "frame"), scatter_dimension=2, tiled=True
        ).astype(jnp.float32),
    )


def score_block(query_block, key_heads):
    return jnp.einsum(
        "qhe,khe->hqk", query_block, key_heads, preferred_element_type=jnp.float32
    ) * HD ** (-0.5)


def clip_views(head_cols, query_rows, key_value):
    head_count = head_cols // HD
    query_total = query_rows.shape[0]
    block_rows = min(512, query_total)
    key_heads = key_value[:, :head_cols].reshape(-1, head_count, HD)
    value_heads = key_value[:, head_cols:].reshape(-1, head_count, HD)
    query_blocks = query_rows.reshape(query_total // block_rows, block_rows, head_count, HD)
    return (query_blocks, key_heads, value_heads)


def attend_clip(head_cols, inputs):
    query_rows, key_value = inputs
    query_blocks, key_heads, value_heads = clip_views(head_cols, query_rows, key_value)

    def one_block(query_block):
        soft_probs = jax.nn.softmax(score_block(query_block, key_heads), axis=-1)
        return to_half(
            jnp.einsum(
                "hqk,khe->qhe", to_half(soft_probs), value_heads, preferred_element_type=jnp.float32
            )
        )

    return lax.map(one_block, query_blocks).reshape(query_rows.shape[0], head_cols)


def attend_clip_back(head_cols, inputs):
    query_rows, key_value, grad_mixed = inputs
    query_blocks, key_heads, value_heads = clip_views(head_cols, query_rows, key_value)
    grad_blocks = grad_mixed.reshape(query_blocks.shape)
    head_count = head_cols // HD

    def one_block(carry, pair_in):
        query_block, grad_block = pair_in
        scores = score_block(query_block, key_heads)
        soft_probs = jax.nn.softmax(scores, axis=-1)
        grad_probs = jnp.einsum(
            "qhe,khe->hqk", grad_block, value_heads, preferred_element_type=jnp.float32
        )
        row_terms = jnp.sum(soft_probs * grad_probs, axis=-1, keepdims=True)
        grad_scores = to_half(soft_probs * (grad_probs - row_terms))
        grad_query = jnp.einsum(
            "hqk,khe->qhe", grad_scores, key_heads, preferred_element_type=jnp.float32
        ) * HD ** (-0.5)
        grad_key = jnp.einsum(
            "hqk,qhe->khe", grad_scores, query_block, preferred_element_type=jnp.float32
        ) * HD ** (-0.5)
        grad_value = jnp.einsum(
            "hqk,qhe->khe", to_half(soft_probs), grad_block, preferred_element_type=jnp.float32
        )
        log_totals = jnp.transpose(jax.nn.logsumexp(scores, axis=-1))
        return (
            (carry[0] + grad_key, carry[1] + grad_value),
            (grad_query, log_totals, jnp.transpose(row_terms[..., 0])),
        )

    zeros_heads = jnp.zeros(key_heads.shape, jnp.float32)
    sums_kv, outs_blocks = lax.scan(
        one_block, (zeros_heads, zeros_heads), (query_blocks, grad_blocks)
    )
    grad_queries, log_totals, row_terms = outs_blocks
    key_total = key_heads.shape[0]
    query_total = query_rows.shape[0]
    grad_kv = jnp.concatenate(
        [sums_kv[0].reshape(key_total, head_cols), sums_kv[1].reshape(key_total, head_cols)],
        axis=-1,
    )
    return (
        grad_queries.reshape(query_total, head_cols),
        grad_kv,
        log_totals.reshape(query_total, head_count),
        row_terms.reshape(query_total, head_count),
    )


def micro_pass(weights, latent_mb, noise_mb, level_mb, context_mb, frame_ids, token_total):
    w_in, w_outs, w_cond, w_time, w_patch = weights
    head_cols = D // lax.axis_size("tensor")
    w_qkv = w_in[:, : 3 * head_cols]
    w_up = w_in[:, 3 * head_cols :]
    w_out = w_outs[:head_cols]
    w_down = w_outs[head_cols:]
    w_first = w_time[:TEMB]
    w_second = w_time[TEMB:]
    w_embed = w_patch[0]
    w_head = w_patch[1]
    clips_here, frames_here = level_mb.shape
    groups = clips_here * frames_here
    clean_frames = frame_ids[None, :] < context_mb[:, None]
    level_values = jnp.where(clean_frames, 0, level_mb).astype(jnp.float32)
    alpha_coef, sigma_coef = noise_terms(level_values)
    embed_low = to_half(frequency_table(level_values).reshape(groups, TEMB))
    hidden_time = product(embed_low, w_first)
    first_low = to_half(jax.nn.silu(hidden_time))
    cond_vec = product(first_low, w_second)
    cond_low = to_half(jax.nn.silu(cond_vec))
    modulation = lax.all_gather(product(cond_low, w_cond), "tensor", axis=1, tiled=True)
    pieces = [
        modulation[:, None, which_piece * D : (which_piece + 1) * D] for which_piece in range(8)
    ]
    alpha_field = alpha_coef[:, :, None, None]
    sigma_field = sigma_coef[:, :, None, None]
    clean_field = latent_mb.astype(jnp.float32)
    noise_field = noise_mb.astype(jnp.float32)
    noisy_field = alpha_field * clean_field + sigma_field * noise_field
    target = alpha_field * noise_field - sigma_field * clean_field
    patch_low = to_half(patchify(noisy_field).reshape(groups, -1, PD))
    goal_rows = patchify(target).reshape(groups, -1, PD)
    rows_local = patch_low.shape[1]
    residual_in = product(patch_low.reshape(-1, PD), w_embed).reshape(groups, rows_local, D)
    normed_one = modulate(residual_in, pieces[0], pieces[1])
    flat_one = gather_rows(to_half(normed_one)).reshape(-1, D)
    qkv_rows = to_half(product(flat_one, w_qkv)).reshape(clips_here, -1, 3 * head_cols)
    query_rows = qkv_rows[..., :head_cols]
    key_value = lax.all_gather(qkv_rows[..., head_cols:], "frame", axis=1, tiled=True)
    mixed_rows = lax.map(partial(attend_clip, head_cols), (query_rows, key_value))
    mixed_flat = mixed_rows.reshape(-1, head_cols)
    attn_out = scatter_rows(product(mixed_flat, w_out).reshape(groups, -1, D))
    residual_mid = residual_in + pieces[2] * attn_out
    normed_two = modulate(residual_mid, pieces[3], pieces[4])
    flat_two = gather_rows(to_half(normed_two)).reshape(-1, D)
    hidden = product(flat_two, w_up)
    act_low = to_half(jax.nn.gelu(hidden, approximate=True))
    mlp_out = scatter_rows(product(act_low, w_down).reshape(groups, -1, D))
    residual_out = residual_mid + pieces[5] * mlp_out
    final_low = to_half(modulate(residual_out, pieces[6], pieces[7]))
    predicted = cols_product(final_low.reshape(-1, D), w_head).reshape(groups, rows_local, PD)
    weight_rows = (1.0 - clean_frames.astype(jnp.float32)).reshape(groups, 1, 1)
    error_rows = predicted - goal_rows
    loss_part = jnp.sum(weight_rows * error_rows * error_rows) / token_total
    grad_pred = to_half(2.0 * weight_rows * error_rows / token_total).reshape(-1, PD)
    grad_head = rows_product(grad_pred, final_low.reshape(-1, D))
    grad_final = product(grad_pred, w_head).reshape(groups, rows_local, D)
    grad_residual, grad_six, grad_seven = modulate_back(
        residual_out, pieces[6], pieces[7], grad_final
    )
    grad_five = jnp.sum(mlp_out * grad_residual, axis=1, keepdims=True)
    grad_mlp = gather_rows(to_half(pieces[5] * grad_residual)).reshape(-1, D)
    grad_down = rows_product(act_low, grad_mlp)
    grad_act = cols_product(grad_mlp, w_down)
    unused, gelu_back = jax.vjp(partial(jax.nn.gelu, approximate=True), hidden)
    grad_hidden = to_half(gelu_back(grad_act)[0])
    grad_up = rows_product(flat_two, grad_hidden)
    grad_normed = scatter_rows(cols_product(grad_hidden, w_up).reshape(groups, -1, D))
    grad_branch, grad_three, grad_four = modulate_back(
        residual_mid, pieces[3], pieces[4], grad_normed
    )
    grad_residual = grad_residual + grad_branch
    grad_two = jnp.sum(attn_out * grad_residual, axis=1, keepdims=True)
    grad_attn = gather_rows(to_half(pieces[2] * grad_residual)).reshape(-1, D)
    grad_out = rows_product(mixed_flat, grad_attn)
    grad_mixed = to_half(cols_product(grad_attn, w_out)).reshape(clips_here, -1, head_cols)
    grad_query, grad_kv, log_rows, term_rows = lax.map(
        partial(attend_clip_back, head_cols), (query_rows, key_value, grad_mixed)
    )
    grad_kv_local = to_half(
        lax.psum_scatter(
            grad_kv.astype(jnp.bfloat16), "frame", scatter_dimension=1, tiled=True
        ).astype(jnp.float32)
    )
    grad_qkv = jnp.concatenate([to_half(grad_query), grad_kv_local], axis=-1).reshape(
        -1, 3 * head_cols
    )
    grad_wqkv = rows_product(flat_one, grad_qkv)
    grad_normed = scatter_rows(cols_product(grad_qkv, w_qkv).reshape(groups, -1, D))
    grad_branch, grad_zero, grad_one = modulate_back(residual_in, pieces[0], pieces[1], grad_normed)
    grad_residual = grad_residual + grad_branch
    grad_embed = rows_product(patch_low.reshape(-1, PD), to_half(grad_residual).reshape(-1, D))
    grad_mod = jnp.concatenate(
        [grad_zero, grad_one, grad_two, grad_three, grad_four, grad_five, grad_six, grad_seven],
        axis=-1,
    )[:, 0, :]
    grad_mod_low = to_half(
        lax.psum_scatter(
            grad_mod.astype(jnp.bfloat16), "tensor", scatter_dimension=1, tiled=True
        ).astype(jnp.float32)
    )
    grad_wcond = rows_product(cond_low, grad_mod_low)
    grad_cond_part = cols_product(grad_mod_low, w_cond)
    grad_cond_all, grad_patch = (
        lax.psum(grad_cond_part.astype(jnp.bfloat16), "tensor").astype(jnp.float32),
        lax.psum(jnp.stack([grad_embed, grad_head]).astype(jnp.bfloat16), "tensor").astype(
            jnp.float32
        ),
    )
    unused, silu_cond = jax.vjp(jax.nn.silu, cond_vec)
    grad_cond_low = to_half(silu_cond(grad_cond_all)[0])
    grad_second = rows_product(first_low, grad_cond_low)
    grad_first_act = cols_product(grad_cond_low, w_second)
    unused, silu_first = jax.vjp(jax.nn.silu, hidden_time)
    grad_hidden_time = to_half(silu_first(grad_first_act)[0])
    grad_first = rows_product(embed_low, grad_hidden_time)
    grad_set = (
        jnp.concatenate([grad_wqkv, grad_up], axis=1),
        jnp.concatenate([grad_out, grad_down], axis=0),
        grad_wcond,
        jnp.concatenate([grad_first, grad_second], axis=0),
        grad_patch,
    )
    return (grad_set, loss_part)


def adam_update(master, first_old, second_old, grad_in, factor, fix_first, fix_second):
    clipped = grad_in * factor
    first_new = BETA_FIRST * first_old + (1.0 - BETA_FIRST) * clipped
    second_new = BETA_SECOND * second_old + (1.0 - BETA_SECOND) * clipped * clipped
    step_dir = first_new / fix_first / (jnp.sqrt(second_new / fix_second) + ADAM_EPS)
    master_new = master - LEARN_RATE * (step_dir + WEIGHT_DECAY * master)
    return (master_new, first_new, second_new)


def shards(
    latent,
    noise_draw,
    levels,
    context,
    step_count,
    w_in,
    w_outs,
    w_cond,
    w_time,
    w_patch,
    m_in,
    m_outs,
    m_cond,
    m_time,
    m_patch,
    v_in,
    v_outs,
    v_cond,
    v_time,
    v_patch,
):
    masters = (w_in, w_outs, w_cond, w_time, w_patch)
    clips_local = latent.shape[0]
    frames_here = latent.shape[1]
    frame_ids = lax.axis_index("frame") * frames_here + jnp.arange(frames_here, dtype=jnp.int32)
    context_local = lax.dynamic_slice_in_dim(
        context, lax.axis_index("dp") * clips_local, clips_local
    )
    token_total = (TOKF * jnp.sum(FRAMES - context)).astype(jnp.float32)
    half_masters = [to_half(master) for master in masters]
    loss_sum = jnp.zeros((), jnp.float32)
    for batch_index in range(MB):
        weights = fetch_weights(
            half_masters[0], half_masters[1], half_masters[2], half_masters[3], half_masters[4]
        )
        clip_start = batch_index * CLIP_DEV
        clip_stop = clip_start + CLIP_DEV
        grad_set, loss_part = micro_pass(
            weights,
            latent[clip_start:clip_stop],
            noise_draw[clip_start:clip_stop],
            levels[clip_start:clip_stop],
            context_local[clip_start:clip_stop],
            frame_ids,
            token_total,
        )
        loss_sum = loss_sum + loss_part
        accumulated = grad_set if batch_index == 0 else jax.tree.map(jnp.add, accumulated, grad_set)
    final_grads = reduce_grads(accumulated)
    split_square = sum((jnp.sum(grad_in * grad_in) for grad_in in final_grads[:3]))
    shared_square = sum(
        (jnp.sum(grad_in * grad_in) for grad_in in final_grads[3:])
    ) / lax.axis_size("tensor")
    totals = lax.psum((loss_sum, split_square + shared_square), ("dp", "frame", "tensor"))
    loss_value = totals[0]
    grad_norm = jnp.sqrt(totals[1])
    factor = jnp.minimum(1.0, MAX_NORM / (grad_norm + 1e-06))
    steps_done = step_count[0].astype(jnp.float32)
    fix_first = 1.0 - BETA_FIRST**steps_done
    fix_second = 1.0 - BETA_SECOND**steps_done
    firsts = (m_in, m_outs, m_cond, m_time, m_patch)
    seconds = (v_in, v_outs, v_cond, v_time, v_patch)
    results = [
        adam_update(
            masters[which],
            firsts[which],
            seconds[which],
            final_grads[which],
            factor,
            fix_first,
            fix_second,
        )
        for which in range(5)
    ]
    return (
        loss_value,
        grad_norm,
        results[0][0],
        results[1][0],
        results[2][0],
        results[3][0],
        results[4][0],
        results[0][1],
        results[1][1],
        results[2][1],
        results[3][1],
        results[4][1],
        results[0][2],
        results[1][2],
        results[2][2],
        results[3][2],
        results[4][2],
        to_half(results[0][0]),
        to_half(results[1][0]),
        to_half(results[2][0]),
        to_half(results[3][0]),
        to_half(results[4][0]),
    )


def solution(mesh):
    placed = (
        P("dp", "frame", "tensor", None),
        P("dp", "frame", "tensor", None),
        P("dp", "frame"),
        P(),
        P(),
        P(("dp", "frame"), "tensor"),
        P("tensor", ("dp", "frame")),
        P(("dp", "frame"), "tensor"),
        P(("dp", "frame"), None),
        P(None, None, ("dp", "frame")),
        P(("dp", "frame"), "tensor"),
        P("tensor", ("dp", "frame")),
        P(("dp", "frame"), "tensor"),
        P(("dp", "frame"), None),
        P(None, None, ("dp", "frame")),
        P(("dp", "frame"), "tensor"),
        P("tensor", ("dp", "frame")),
        P(("dp", "frame"), "tensor"),
        P(("dp", "frame"), None),
        P(None, None, ("dp", "frame")),
    )
    return jax.shard_map(
        shards,
        mesh=mesh,
        in_specs=placed,
        out_specs=(
            P(),
            P(),
            P(("dp", "frame"), "tensor"),
            P("tensor", ("dp", "frame")),
            P(("dp", "frame"), "tensor"),
            P(("dp", "frame"), None),
            P(None, None, ("dp", "frame")),
            P(("dp", "frame"), "tensor"),
            P("tensor", ("dp", "frame")),
            P(("dp", "frame"), "tensor"),
            P(("dp", "frame"), None),
            P(None, None, ("dp", "frame")),
            P(("dp", "frame"), "tensor"),
            P("tensor", ("dp", "frame")),
            P(("dp", "frame"), "tensor"),
            P(("dp", "frame"), None),
            P(None, None, ("dp", "frame")),
            P(("dp", "frame"), "tensor"),
            P("tensor", ("dp", "frame")),
            P(("dp", "frame"), "tensor"),
            P(("dp", "frame"), None),
            P(None, None, ("dp", "frame")),
        ),
        check_vma=False,
    )
```

profile of v0, /device:TPU:0, one launch (start us, length us, event | category | flops | bytes accessed | tf_op | source)
XLA Modules:
  0.0 3935.1 jit_solution(3038980276749586682)
XLA Ops:
  46.7 36.0 all-gather.22.cloned.1.call-done
  149.0 56.2 %all-gather.40.cloned.1.call-done = bf16[8,256,1024]{2,1,0:T(8,128)(2,1)} async-done(((bf16[8,64,1024]{2,1,0:T(8,128)(2,1)}), bf16[8,256,1024]{2,1,0:T(8,128)(2,1)}) %all-gather.40.cloned.1.call-update) | async-done | bytes 4194320 | tf_op jit(solution)/shard_map/all_gather | solution.py:97
  215.5 70.6 %all-gather.24.cloned.1.call-done = bf16[8,256,1024]{2,1,0:T(8,128)(2,1)} async-done(((bf16[8,64,1024]{2,1,0:T(8,128)(2,1)}), bf16[8,256,1024]{2,1,0:T(8,128)(2,1)}) %all-gather.24.cloned.1.call-update) | async-done | bytes 4194320 | tf_op jit(solution)/shard_map/all_gather | solution.py:97
  300.2 67.2 %all-gather.34.cloned.1.call-done = bf16[8,256,1024]{2,1,0:T(8,128)(2,1)} async-done(((bf16[8,64,1024]{2,1,0:T(8,128)(2,1)}), bf16[8,256,1024]{2,1,0:T(8,128)(2,1)}) %all-gather.34.cloned.1.call-update) | async-done | bytes 4194320 | tf_op jit(solution)/shard_map/all_gather | solution.py:97
  377.2 47.1 %all-gather.42.cloned.1.call-done = bf16[1,4096,512]{2,1,0:T(8,128)(2,1)} async-done(((bf16[1,2048,512]{2,1,0:T(8,128)(2,1)}), bf16[1,4096,512]{2,1,0:T(8,128)(2,1)}) %all-gather.42.cloned.1.call-update) | async-done | bytes 4194320 | tf_op jit(solution)/shard_map/all_gather | solution.py:255
  434.1 97.3 %while.128 = (s32[]{:T(128)}, bf16[4,512,4,64]{1,3,2,0:T(8,128)(2,1)S(1)}, bf16[4,512,4,64]{1,3,2,0:T(8,128)(2,1)}, bf16[4096,4,64]{0,2,1:T(8,128)(2,1)S(1)}, bf16[4096,4,64]{0,2,1:T(8,128)(2,1)}, /*index=5*/s32[]{:T(128)}) while((s32[]{:T(128)}, bf16[4,512,4,64]{1,3,2,0:T(8,128)(2,1)S(1)}, bf16[4,512,4,64]{1,3,2,0:T(8,128)(2,1)}, ...), condition=%wide.region_32.33_spmd, body=%wide.region_29.32_spmd.sunk | while | flops 3280087040 | bytes 7095377 | solution.py:164
  557.9 97.0 %while.126 = (s32[]{:T(128)}, bf16[4,512,4,64]{1,3,2,0:T(8,128)(2,1)S(1)}, bf16[4,512,4,64]{1,3,2,0:T(8,128)(2,1)}, bf16[4096,4,64]{0,2,1:T(8,128)(2,1)S(1)}, bf16[4096,4,64]{0,2,1:T(8,128)(2,1)}, /*index=5*/s32[]{:T(128)}) while((s32[]{:T(128)}, bf16[4,512,4,64]{1,3,2,0:T(8,128)(2,1)S(1)}, bf16[4,512,4,64]{1,3,2,0:T(8,128)(2,1)}, ...), condition=%wide.region_5.6_spmd, body=%wide.region_2.0_spmd.sunk | while | flops 3280087040 | bytes 7095377 | solution.py:164
  682.2 97.0 %while.127 = (s32[]{:T(128)}, bf16[4,512,4,64]{1,3,2,0:T(8,128)(2,1)S(1)}, bf16[4,512,4,64]{1,3,2,0:T(8,128)(2,1)}, bf16[4096,4,64]{0,2,1:T(8,128)(2,1)S(1)}, bf16[4096,4,64]{0,2,1:T(8,128)(2,1)}, /*index=5*/s32[]{:T(128)}) while((s32[]{:T(128)}, bf16[4,512,4,64]{1,3,2,0:T(8,128)(2,1)S(1)}, bf16[4,512,4,64]{1,3,2,0:T(8,128)(2,1)}, ...), condition=%wide.region_19.20_spmd, body=%wide.region_16.19_spmd.sunk | while | flops 3280087040 | bytes 7095377 | solution.py:164
  803.1 64.6 %reduce-scatter.34.cloned.1.call-done = bf16[8,64,1024]{2,1,0:T(8,128)(2,1)} async-done(((bf16[8,256,1024]{2,1,0:T(8,128)(2,1)}), bf16[8,64,1024]{2,1,0:T(8,128)(2,1)}) %reduce-scatter.34.cloned.1.call-update) | async-done | bytes 1048592 | tf_op jit(solution)/shard_map/reduce_scatter | solution.py:101
  873.0 77.5 %all-gather.44.cloned.1.call-done = bf16[8,256,1024]{2,1,0:T(8,128)(2,1)} async-done(((bf16[8,64,1024]{2,1,0:T(8,128)(2,1)}), bf16[8,256,1024]{2,1,0:T(8,128)(2,1)}) %all-gather.44.cloned.1.call-update) | async-done | bytes 4194320 | tf_op jit(solution)/shard_map/all_gather | solution.py:97
  964.3 67.5 %all-gather.32.cloned.1.call-done = bf16[8,256,1024]{2,1,0:T(8,128)(2,1)} async-done(((bf16[8,64,1024]{2,1,0:T(8,128)(2,1)}), bf16[8,256,1024]{2,1,0:T(8,128)(2,1)}) %all-gather.32.cloned.1.call-update) | async-done | bytes 4194320 | tf_op jit(solution)/shard_map/all_gather | solution.py:97
  1045.9 66.8 %all-gather.38.cloned.1.call-done = bf16[8,256,1024]{2,1,0:T(8,128)(2,1)} async-done(((bf16[8,64,1024]{2,1,0:T(8,128)(2,1)}), bf16[8,256,1024]{2,1,0:T(8,128)(2,1)}) %all-gather.38.cloned.1.call-update) | async-done | bytes 4194320 | tf_op jit(solution)/shard_map/all_gather | solution.py:97
  1129.8 60.5 %reduce-scatter.40.cloned.1.call-done = bf16[8,64,1024]{2,1,0:T(8,128)(2,1)} async-done(((bf16[8,256,1024]{2,1,0:T(8,128)(2,1)}), bf16[8,64,1024]{2,1,0:T(8,128)(2,1)}) %reduce-scatter.40.cloned.1.call-update) | async-done | bytes 1048592 | tf_op jit(solution)/shard_map/reduce_scatter | solution.py:101
  1202.2 67.5 %reduce-scatter.32.cloned.1.call-done = bf16[8,64,1024]{2,1,0:T(8,128)(2,1)} async-done(((bf16[8,256,1024]{2,1,0:T(8,128)(2,1)}), bf16[8,64,1024]{2,1,0:T(8,128)(2,1)}) %reduce-scatter.32.cloned.1.call-update) | async-done | bytes 1048592 | tf_op jit(solution)/shard_map/reduce_scatter | solution.py:101
  1281.1 68.4 %reduce-scatter.36.cloned.1.call-done = bf16[8,64,1024]{2,1,0:T(8,128)(2,1)} async-done(((bf16[8,256,1024]{2,1,0:T(8,128)(2,1)}), bf16[8,64,1024]{2,1,0:T(8,128)(2,1)}) %reduce-scatter.36.cloned.1.call-update) | async-done | bytes 1048592 | tf_op jit(solution)/shard_map/reduce_scatter | solution.py:101
  1359.0 73.2 %all-gather.54.cloned.1.call-done = bf16[8,256,1024]{2,1,0:T(8,128)(2,1)} async-done(((bf16[8,64,1024]{2,1,0:T(8,128)(2,1)}), bf16[8,256,1024]{2,1,0:T(8,128)(2,1)}) %all-gather.54.cloned.1.call-update) | async-done | bytes 4194320 | tf_op jit(solution)/shard_map/all_gather | solution.py:97
  1452.4 61.2 %all-gather.46.cloned.1.call-done = bf16[8,256,1024]{2,1,0:T(8,128)(2,1)} async-done(((bf16[8,64,1024]{2,1,0:T(8,128)(2,1)}), bf16[8,256,1024]{2,1,0:T(8,128)(2,1)}) %all-gather.46.cloned.1.call-update) | async-done | bytes 4194320 | tf_op jit(solution)/shard_map/all_gather | solution.py:97
  1533.9 60.6 %all-gather.50.cloned.1.call-done = bf16[8,256,1024]{2,1,0:T(8,128)(2,1)} async-done(((bf16[8,64,1024]{2,1,0:T(8,128)(2,1)}), bf16[8,256,1024]{2,1,0:T(8,128)(2,1)}) %all-gather.50.cloned.1.call-update) | async-done | bytes 4194320 | tf_op jit(solution)/shard_map/all_gather | solution.py:97
  1614.6 57.5 %reduce-scatter.50.cloned.1.call-done = bf16[8,64,1024]{2,1,0:T(8,128)(2,1)} async-done(((bf16[8,256,1024]{2,1,0:T(8,128)(2,1)}), bf16[8,64,1024]{2,1,0:T(8,128)(2,1)}) %reduce-scatter.50.cloned.1.call-update) | async-done | bytes 1048592 | tf_op jit(solution)/shard_map/reduce_scatter | solution.py:101
  1682.8 68.9 %reduce-scatter.42.cloned.1.call-done = bf16[8,64,1024]{2,1,0:T(8,128)(2,1)} async-done(((bf16[8,256,1024]{2,1,0:T(8,128)(2,1)}), bf16[8,64,1024]{2,1,0:T(8,128)(2,1)}) %reduce-scatter.42.cloned.1.call-update) | async-done | bytes 1048592 | tf_op jit(solution)/shard_map/reduce_scatter | solution.py:101
  1762.0 69.3 %reduce-scatter.46.cloned.1.call-done = bf16[8,64,1024]{2,1,0:T(8,128)(2,1)} async-done(((bf16[8,256,1024]{2,1,0:T(8,128)(2,1)}), bf16[8,64,1024]{2,1,0:T(8,128)(2,1)}) %reduce-scatter.46.cloned.1.call-update) | async-done | bytes 1048592 | tf_op jit(solution)/shard_map/reduce_scatter | solution.py:101
  1839.5 74.6 %all-gather.56.cloned.1.call-done = bf16[8,256,1024]{2,1,0:T(8,128)(2,1)} async-done(((bf16[8,64,1024]{2,1,0:T(8,128)(2,1)}), bf16[8,256,1024]{2,1,0:T(8,128)(2,1)}) %all-gather.56.cloned.1.call-update) | async-done | bytes 4194320 | tf_op jit(solution)/shard_map/all_gather | solution.py:97
  1924.8 412.1 %while.131 = (s32[]{:T(128)}, f32[4096,4,64]{0,2,1:T(8,128)}, f32[4096,4,64]{0,2,1:T(8,128)}, bf16[4,512,4,64]{1,3,2,0:T(8,128)(2,1)}, bf16[4,512,4,64]{1,3,2,0:...) while((s32[]{:T(128)}, f32[4096,4,64]{0,2,1:T(8,128)}, ...), condition=%wide.region_72.73_spmd.clone, body=%wide.region_68.72_spmd.clone.sunk | while | flops 6565273600 | bytes 312264384 | solution.py:198
  2360.2 410.5 %while.129 = (s32[]{:T(128)}, f32[4096,4,64]{0,2,1:T(8,128)}, f32[4096,4,64]{0,2,1:T(8,128)}, bf16[4,512,4,64]{1,3,2,0:T(8,128)(2,1)}, bf16[4,512,4,64]{1,3,2,0:...) while((s32[]{:T(128)}, f32[4096,4,64]{0,2,1:T(8,128)}, ...), condition=%wide.region_50.51_spmd.clone, body=%wide.region_46.50_spmd.clone.sunk | while | flops 6565273600 | bytes 312264384 | solution.py:198
  2793.8 410.7 %while.130 = (s32[]{:T(128)}, f32[4096,4,64]{0,2,1:T(8,128)}, f32[4096,4,64]{0,2,1:T(8,128)}, bf16[4,512,4,64]{1,3,2,0:T(8,128)(2,1)}, bf16[4,512,4,64]{1,3,2,0:...) while((s32[]{:T(128)}, f32[4096,4,64]{0,2,1:T(8,128)}, ...), condition=%wide.region_61.62_spmd.clone, body=%wide.region_57.61_spmd.clone.sunk | while | flops 6565273600 | bytes 312264384 | solution.py:198
  3352.8 78.1 %reduce-scatter.54.cloned.1.call-done = bf16[8,64,1024]{2,1,0:T(8,128)(2,1)} async-done(((bf16[8,256,1024]{2,1,0:T(8,128)(2,1)}), bf16[8,64,1024]{2,1,0:T(8,128)(2,1)}) %reduce-scatter.54.cloned.1.call-update) | async-done | bytes 1048592 | tf_op jit(solution)/shard_map/reduce_scatter | solution.py:101
  3441.5 69.0 %reduce-scatter.58.cloned.1.call-done = bf16[8,64,1024]{2,1,0:T(8,128)(2,1)} async-done(((bf16[8,256,1024]{2,1,0:T(8,128)(2,1)}), bf16[8,64,1024]{2,1,0:T(8,128)(2,1)}) %reduce-scatter.58.cloned.1.call-update) | async-done | bytes 1048592 | tf_op jit(solution)/shard_map/reduce_scatter | solution.py:101
  3687.4 38.9 reduce-scatter.70.cloned.1.call-done
  3729.8 33.8 reduce-scatter.74.cloned.1.call-done
  3765.1 45.8 %reduce-scatter.68.cloned.1.call-done = bf16[160,1024]{1,0:T(8,128)(2,1)} async-done(((bf16[1280,1024]{1,0:T(8,128)(2,1)}), bf16[160,1024]{1,0:T(8,128)(2,1)}) %reduce-scatter.68.cloned.1.call-update) | async-done | bytes 327696 | tf_op jit(solution)/shard_map/reduce_scatter | solution.py:127
  3814.0 51.9 %reduce-scatter.66.cloned.1.call-done = bf16[128,2048]{1,0:T(8,128)(2,1)} async-done(((bf16[1024,2048]{1,0:T(8,128)(2,1)}), bf16[128,2048]{1,0:T(8,128)(2,1)}) %reduce-scatter.66.cloned.1.call-update) | async-done | bytes 524304 | tf_op jit(solution)/shard_map/reduce_scatter | solution.py:124
  3868.5 39.3 all-reduce
  (1157 shorter events, 2333.8 us)
Async XLA Ops:
  12.3 193.0 %all-gather.40.cloned.1.call-start = ((), (), s32[]{:S(2)}) async-start(), calls=%async_computation.37 | async-start | bytes 5242880 | tf_op jit(solution)/shard_map/all_gather | solution.py:97
  101.7 184.4 %all-gather.24.cloned.1.call-start = ((), (), s32[]{:S(2)}) async-start(), calls=%async_computation.25 | async-start | bytes 5242880 | tf_op jit(solution)/shard_map/all_gather | solution.py:97
  124.1 243.4 %all-gather.34.cloned.1.call-start = ((), (), s32[]{:S(2)}) async-start(), calls=%async_computation.32 | async-start | bytes 5242880 | tf_op jit(solution)/shard_map/all_gather | solution.py:97
  148.8 275.5 %all-gather.42.cloned.1.call-start = ((), (), s32[]{:S(2)}) async-start(), calls=%async_computation.38 | async-start | bytes 6291456 | tf_op jit(solution)/shard_map/all_gather | solution.py:255
  214.6 324.4 %all-gather.30.cloned.1.call-start = ((), (), s32[]{:S(2)}) async-start(), calls=%async_computation.28 | async-start | bytes 2949120 | tf_op jit(solution)/shard_map/all_gather | solution.py:109
  215.5 332.7 %all-gather.28.cloned.1.call-start = ((), (), s32[]{:S(2)}) async-start(), calls=%async_computation.27 | async-start | bytes 6291456 | tf_op jit(solution)/shard_map/all_gather | solution.py:255
  295.6 376.2 %all-gather.36.cloned.1.call-start = ((), (), s32[]{:S(2)}) async-start(), calls=%async_computation.33 | async-start | bytes 6291456 | tf_op jit(solution)/shard_map/all_gather | solution.py:255
  376.8 414.7 %reduce-scatter.38.cloned.1.call-start = ((), (), s32[]{:S(2)}) async-start(), calls=%async_computation.39 | async-start | bytes 5242880 | tf_op jit(solution)/shard_map/reduce_scatter | solution.py:101
  543.8 254.2 %reduce-scatter.30.cloned.1.call-start = ((), (), s32[]{:S(2)}) async-start(), calls=%async_computation.29 | async-start | bytes 5242880 | tf_op jit(solution)/shard_map/reduce_scatter | solution.py:101
  667.4 200.3 %reduce-scatter.34.cloned.1.call-start = ((), (), s32[]{:S(2)}) async-start(), calls=%async_computation.34 | async-start | bytes 5242880 | tf_op jit(solution)/shard_map/reduce_scatter | solution.py:101
  797.9 233.9 %all-gather.32.cloned.1.call-start = ((), (), s32[]{:S(2)}) async-start(), calls=%async_computation.30 | async-start | bytes 5242880 | tf_op jit(solution)/shard_map/all_gather | solution.py:97
  803.0 309.7 %all-gather.38.cloned.1.call-start = ((), (), s32[]{:S(2)}) async-start(), calls=%async_computation.35 | async-start | bytes 5242880 | tf_op jit(solution)/shard_map/all_gather | solution.py:97
  872.9 317.3 %reduce-scatter.40.cloned.1.call-start = ((), (), s32[]{:S(2)}) async-start(), calls=%async_computation.41 | async-start | bytes 5242880 | tf_op jit(solution)/shard_map/reduce_scatter | solution.py:101
  964.3 305.4 %reduce-scatter.32.cloned.1.call-start = ((), (), s32[]{:S(2)}) async-start(), calls=%async_computation.31 | async-start | bytes 5242880 | tf_op jit(solution)/shard_map/reduce_scatter | solution.py:101
  1045.8 303.6 %reduce-scatter.36.cloned.1.call-start = ((), (), s32[]{:S(2)}) async-start(), calls=%async_computation.36 | async-start | bytes 5242880 | tf_op jit(solution)/shard_map/reduce_scatter | solution.py:101
  1126.5 305.7 %all-gather.54.cloned.1.call-start = ((), (), s32[]{:S(2)}) async-start(), calls=%async_computation.50 | async-start | bytes 5242880 | tf_op jit(solution)/shard_map/all_gather | solution.py:97
  1200.3 313.3 %all-gather.46.cloned.1.call-start = ((), (), s32[]{:S(2)}) async-start(), calls=%async_computation.42 | async-start | bytes 5242880 | tf_op jit(solution)/shard_map/all_gather | solution.py:97
  1279.6 315.0 %all-gather.50.cloned.1.call-start = ((), (), s32[]{:S(2)}) async-start(), calls=%async_computation.46 | async-start | bytes 5242880 | tf_op jit(solution)/shard_map/all_gather | solution.py:97
  1358.8 313.4 %reduce-scatter.50.cloned.1.call-start = ((), (), s32[]{:S(2)}) async-start(), calls=%async_computation.51 | async-start | bytes 5242880 | tf_op jit(solution)/shard_map/reduce_scatter | solution.py:101
  1452.1 299.6 %reduce-scatter.42.cloned.1.call-start = ((), (), s32[]{:S(2)}) async-start(), calls=%async_computation.43 | async-start | bytes 5242880 | tf_op jit(solution)/shard_map/reduce_scatter | solution.py:101
  1533.6 297.7 %reduce-scatter.46.cloned.1.call-start = ((), (), s32[]{:S(2)}) async-start(), calls=%async_computation.47 | async-start | bytes 5242880 | tf_op jit(solution)/shard_map/reduce_scatter | solution.py:101
  1614.6 299.6 %all-gather.56.cloned.1.call-start = ((), (), s32[]{:S(2)}) async-start(), calls=%async_computation.52 | async-start | bytes 5242880 | tf_op jit(solution)/shard_map/all_gather | solution.py:97
  1682.3 664.5 %all-gather.48.cloned.1.call-start = ((), (), s32[]{:S(2)}) async-start(), calls=%async_computation.44 | async-start | bytes 5242880 | tf_op jit(solution)/shard_map/all_gather | solution.py:97
  1761.9 1018.7 %all-gather.52.cloned.1.call-start = ((), (), s32[]{:S(2)}) async-start(), calls=%async_computation.48 | async-start | bytes 5242880 | tf_op jit(solution)/shard_map/all_gather | solution.py:97
  1839.5 1383.7 %reduce-scatter.52.cloned.1.call-start = ((), (), s32[]{:S(2)}) async-start(), calls=%async_computation.53 | async-start | bytes 6291456 | tf_op jit(solution)/shard_map/reduce_scatter | solution.py:297
  2358.2 877.0 %reduce-scatter.44.cloned.1.call-start = ((), (), s32[]{:S(2)}) async-start(), calls=%async_computation.45 | async-start | bytes 6291456 | tf_op jit(solution)/shard_map/reduce_scatter | solution.py:297
  2791.9 480.3 %reduce-scatter.48.cloned.1.call-start = ((), (), s32[]{:S(2)}) async-start(), calls=%async_computation.49 | async-start | bytes 6291456 | tf_op jit(solution)/shard_map/reduce_scatter | solution.py:297
  3231.3 199.6 %reduce-scatter.54.cloned.1.call-start = ((), (), s32[]{:S(2)}) async-start(), calls=%async_computation.54 | async-start | bytes 5242880 | tf_op jit(solution)/shard_map/reduce_scatter | solution.py:101
  3242.9 267.6 %reduce-scatter.58.cloned.1.call-start = ((), (), s32[]{:S(2)}) async-start(), calls=%async_computation.56 | async-start | bytes 5242880 | tf_op jit(solution)/shard_map/reduce_scatter | solution.py:101
  3279.7 309.1 %all-reduce.5.cloned.1.call-start = ((), (), s32[]{:S(2)}) async-start(), calls=%async_computation.65 | async-start | bytes 393216 | tf_op jit(solution)/shard_map/psum | solution.py:322
  3591.2 219.8 %reduce-scatter.68.cloned.1.call-start = ((), (), s32[]{:S(2)}) async-start(), calls=%async_computation.61 | async-start | bytes 2949120 | tf_op jit(solution)/shard_map/reduce_scatter | solution.py:127
  3670.6 195.3 %reduce-scatter.66.cloned.1.call-start = ((), (), s32[]{:S(2)}) async-start(), calls=%async_computation.60 | async-start | bytes 4718592 | tf_op jit(solution)/shard_map/reduce_scatter | solution.py:124
  (323 other events, 5838.5 us)
Sparse Core Ops, SparseCore 0:
  121.8 83.4 all-gather.39
  207.3 78.8 all-gather.23
  288.1 79.2 all-gather.33
  369.0 55.2 all-gather.41
  458.9 56.7 all-gather.27
  517.0 56.7 all-gather.35
  576.1 76.7 reduce-scatter.37
  667.5 76.6 reduce-scatter.29
  791.5 76.1 reduce-scatter.33
  869.2 81.2 all-gather.43
  952.5 79.2 all-gather.31
  1033.4 79.2 all-gather.37
  1114.9 75.2 reduce-scatter.39
  1192.4 77.2 reduce-scatter.31
  1272.1 77.2 reduce-scatter.35
  1350.8 81.2 all-gather.53
  1434.3 79.2 all-gather.45
  1515.2 79.2 all-gather.49
  1596.8 75.2 reduce-scatter.49
  1674.4 77.2 reduce-scatter.41
  1754.0 77.2 reduce-scatter.45
  1832.8 81.2 all-gather.55
  1916.2 79.2 all-gather.47
  1997.2 79.2 all-gather.51
  2358.3 52.7 reduce-scatter.51
  2792.0 52.8 reduce-scatter.43
  3219.3 52.9 reduce-scatter.47
  3274.5 76.7 reduce-scatter.61
  3353.6 77.2 reduce-scatter.53
  3433.2 77.2 reduce-scatter.57
  3677.6 48.6 reduce-scatter.69
  3814.5 51.3 reduce-scatter.65
  (11 shorter events, 342.5 us)
where the time goes:
time: 3950 us; the launch traced here: 3940 us
  waiting for transfers between devices  1610 us (41%)
  matrix products  1480 us (37%)
  other arithmetic  491 us (12%)
  local copies, waits for them, and re-layouts  206 us (5%)
  blocking collectives  119 us (3%)
    all_gather x12, waiting for transfers between devices, gather_rows(): return lax.all_gather(array_in, 'tensor', axis=1, tiled=True)  676 us
    reduce_scatter x12, waiting for transfers between devices, scatter_rows(): lax.psum_scatter(array_in.astype(jnp.bfloat16), 'tensor', scatter_dimensi...  634 us
    convert_element_type x32, other arithmetic, to_half(): return array_in.astype(jnp.bfloat16)  362 us
    dot_general x12, matrix products, one_block(): jnp.einsum('qhe,khe->hqk', grad_block, value_heads, preferred_element_typ...  310 us
    sub x12, matrix products, one_block(): soft_probs = jax.nn.softmax(scores, axis=-1)  205 us
    dot_general x12, matrix products, one_block(): jnp.einsum('hqk,qhe->khe', to_half(soft_probs), grad_block, preferred_ele...  172 us
    dot_general x12, matrix products, one_block(): jnp.einsum('hqk,khe->qhe', to_half(soft_probs), value_heads, preferred_el...  157 us
    sub x12, matrix products, one_block(): soft_probs = jax.nn.softmax(score_block(query_block, key_heads), axis=-1)  134 us
  transfers between devices with their start and end apart: 43, of which 30 were waited for; matrix products, arithmetic and copies ran while one was open for 53% of the time, Pallas kernels for 0%

commit v1 on v0

v1 whole, which is shorter than its diff:
```python
from functools import partial
import math

import jax
import jax.numpy as jnp
from jax import lax
from jax.experimental import pallas as pl
from jax.experimental.pallas import tpu as pltpu
from jax.sharding import PartitionSpec as P

D = 1024
HD = 64
TEMB = 256
CHANNELS = 4
PATCH = 2
PD = 16
TOKF = 256
FRAMES = 16
NLEV = 1000
PAIR = 2 * HD
PLANE = ("dp", "frame")
EVERY = ("tensor", "dp", "frame")
SCORE_SCALE = HD ** (-0.5) * math.log2(math.e)
TOTAL_LOW = 2.0**-40
TOTAL_HIGH = 2.0**70


EPS_NORM = 1e-06
MAX_NORM = 0.1
LEARN_RATE = 0.08
WEIGHT_DECAY = 0.1
BETA_FIRST = 0.5
BETA_SECOND = 0.5
ADAM_EPS = 1e-08


def to_half(array_in):
    return array_in.astype(jnp.bfloat16)


def product(left_mat, right_mat):
    return jnp.dot(left_mat, right_mat, preferred_element_type=jnp.float32)


def rows_product(left_mat, right_mat):
    return lax.dot_general(
        left_mat, right_mat, (((0,), (0,)), ((), ())), preferred_element_type=jnp.float32
    )


def cols_product(left_mat, right_mat):
    return lax.dot_general(
        left_mat, right_mat, (((1,), (1,)), ((), ())), preferred_element_type=jnp.float32
    )


def frequency_table(level_values):
    half_width = TEMB // 2
    rate_table = jnp.exp(
        -math.log(10000.0) * jnp.arange(half_width, dtype=jnp.float32) / half_width
    )
    angles = level_values[..., None] * rate_table
    return jnp.concatenate([jnp.cos(angles), jnp.sin(angles)], axis=-1)


def noise_terms(level_values):
    angles = level_values * (0.5 * math.pi / NLEV)
    return (jnp.cos(angles), jnp.sin(angles))


def modulate(residual, shift_rows, scale_rows):
    centre = residual - jnp.mean(residual, axis=-1, keepdims=True)
    spread = jnp.mean(centre * centre, axis=-1, keepdims=True)
    return centre * lax.rsqrt(spread + EPS_NORM) * (1.0 + scale_rows) + shift_rows


def modulate_back(residual, shift_rows, scale_rows, grad_out):
    unused, pullback = jax.vjp(modulate, residual, shift_rows, scale_rows)
    return pullback(grad_out)


def patchify(field_in):
    lead_shape = field_in.shape[:-2]
    rows_here = field_in.shape[-2]
    width_cells = field_in.shape[-1] // CHANNELS
    lead_rank = len(lead_shape)
    blocks_view = field_in.reshape(
        lead_shape + (rows_here // PATCH, PATCH, width_cells // PATCH, PATCH, CHANNELS)
    )
    order_axes = tuple(range(lead_rank)) + (
        lead_rank,
        lead_rank + 2,
        lead_rank + 1,
        lead_rank + 3,
        lead_rank + 4,
    )
    return jnp.transpose(blocks_view, order_axes).reshape(
        lead_shape + (rows_here // PATCH * (width_cells // PATCH), PATCH * PATCH * CHANNELS)
    )


def contract(left_mat, right_mat, left_dim, right_dim):
    return lax.dot_general(
        left_mat,
        right_mat,
        (((left_dim,), (right_dim,)), ((), ())),
        preferred_element_type=jnp.float32,
    )


def head_lanes(head):
    return lax.broadcasted_iota(jnp.int32, (1, PAIR), 1) // HD == head


def attend_kernel(chunk, query_ref, key_ref, value_ref, exps_ref, low_ref, mixed_ref, inverse_ref):
    key_total = key_ref.shape[1]
    block_rows = query_ref.shape[1]
    query_pair = query_ref[0]
    mixed_parts = []
    inverse_parts = []
    for head in range(2):
        lanes = head_lanes(head)
        query_head = jnp.where(lanes, query_pair, jnp.zeros_like(query_pair))

        def scores_of(rows):
            return contract(key_ref[0, rows, :], query_head, 1, 1) * SCORE_SCALE

        def add_chunk(rows, scores, total):
            exps = jnp.exp2(scores).astype(jnp.bfloat16)
            exps_ref[0, head, :, rows] = exps.T
            values = value_ref[0, rows, :]
            values = jnp.where(lanes, values, jnp.ones_like(values))
            return total + contract(values, exps, 0, 0)

        zeros = jnp.zeros((PAIR, block_rows), jnp.float32)
        total = zeros
        for start in range(0, key_total, chunk):
            rows = slice(start, start + chunk)
            total = add_chunk(rows, scores_of(rows), total)
        sum_rows = total[(1 - head) * HD : (1 - head) * HD + 8]
        outside = jnp.max(
            jnp.where((sum_rows > TOTAL_LOW) & (sum_rows < TOTAL_HIGH), 0.0, 1.0)
        )

        def shifted(unused):
            def chunk_rows(step):
                return pl.ds(pl.multiple_of(step * chunk, chunk), chunk)

            def highest(step, top):
                return jnp.maximum(
                    top, jnp.max(scores_of(chunk_rows(step)), axis=0, keepdims=True)
                )

            top = lax.fori_loop(
                0, key_total // chunk, highest, jnp.full((1, block_rows), -jnp.inf, jnp.float32)
            )

            def one_chunk(step, total):
                rows = chunk_rows(step)
                return add_chunk(rows, scores_of(rows) - top, total)

            return lax.fori_loop(0, key_total // chunk, one_chunk, zeros)

        total = lax.cond(outside > 0.0, shifted, lambda kept: kept, total)
        inverse = 1.0 / total[(1 - head) * HD : (2 - head) * HD]
        mixed_parts.append(total[head * HD : (head + 1) * HD] * inverse)
        inverse_parts.append(inverse)
    mixed = jnp.concatenate(mixed_parts, axis=0).T
    mixed_ref[0] = mixed
    low_ref[0] = mixed.astype(jnp.bfloat16)
    inverse_ref[0] = jnp.concatenate(inverse_parts, axis=0).T


def attend(query_in, key_value, key_place):
    units, query_total = query_in.shape[:2]
    key_total = key_value.shape[1]
    block_rows = min(1024, query_total)
    chunk = min(1024, key_total)

    def query_map(unit, step):
        return (unit, step, 0)

    query_spec = pl.BlockSpec((1, block_rows, PAIR), query_map)
    shape_rows = (units, query_total, PAIR)
    products = 4 * units * query_total * key_total * PAIR
    return pl.pallas_call(
        partial(attend_kernel, chunk),
        grid=(units, query_total // block_rows),
        in_specs=[
            query_spec,
            pl.BlockSpec((1, key_total, PAIR), lambda unit, step: (unit, 0, key_place)),
            pl.BlockSpec((1, key_total, PAIR), lambda unit, step: (unit, 0, key_place + 1)),
        ],
        out_specs=[
            pl.BlockSpec((1, 2, block_rows, key_total), lambda unit, step: (unit, 0, step, 0)),
            query_spec,
            query_spec,
            query_spec,
        ],
        out_shape=[
            jax.ShapeDtypeStruct((units, 2, query_total, key_total), jnp.bfloat16),
            jax.ShapeDtypeStruct(shape_rows, jnp.bfloat16),
            jax.ShapeDtypeStruct(shape_rows, jnp.float32),
            jax.ShapeDtypeStruct(shape_rows, jnp.float32),
        ],
        cost_estimate=pl.CostEstimate(
            flops=4 * products,
            bytes_accessed=4 * units * query_total * key_total,
            transcendentals=2 * units * query_total * key_total,
        ),
        compiler_params=pltpu.CompilerParams(vmem_limit_bytes=62 << 20),
    )(query_in, key_value, key_value)


def attend_back_kernel(
    chunk,
    exps_ref,
    query_ref,
    key_ref,
    value_ref,
    grad_ref,
    mixed_ref,
    inverse_ref,
    grad_query_ref,
    grad_key_ref,
    grad_value_ref,
    key_sums,
    value_sums,
):
    step = pl.program_id(1)
    head = pl.program_id(2)
    key_total = key_ref.shape[1]
    block_rows = query_ref.shape[1]
    lane = lax.broadcasted_iota(jnp.int32, (1, PAIR), 1)
    lanes = head_lanes(head)
    grad_low = jnp.where(lanes, grad_ref[0].astype(jnp.float32) * inverse_ref[0], 0.0).astype(
        jnp.bfloat16
    )
    row_terms = jnp.sum(grad_low.astype(jnp.float32) * mixed_ref[0], axis=1, keepdims=True)
    term_high = row_terms.astype(jnp.bfloat16).astype(jnp.float32)
    term_rest = row_terms - term_high
    term_lanes = jnp.where(lane == 0, -term_high, jnp.where(lane == 1, -term_rest, 0.0))
    grad_wide = jnp.concatenate([grad_low, term_lanes.astype(jnp.bfloat16)], axis=1)
    query_pair = query_ref[0]
    query_columns = jnp.where(lanes, query_pair, jnp.zeros_like(query_pair)).T
    grad_columns = grad_low.T
    term_ones = jnp.broadcast_to(jnp.where(lane < 2, 1.0, 0.0).astype(jnp.bfloat16), (chunk, PAIR))

    @pl.when((step == 0) & (head == 0))
    def start_sums():
        key_sums[...] = jnp.zeros_like(key_sums)
        value_sums[...] = jnp.zeros_like(value_sums)

    grad_query = jnp.zeros((block_rows, PAIR), jnp.float32)
    for start in range(0, key_total, chunk):
        rows = slice(start, start + chunk)
        values_wide = jnp.concatenate([value_ref[0, rows, :], term_ones], axis=1)
        grad_probs = contract(grad_wide, values_wide, 1, 1).astype(jnp.bfloat16)
        exps = exps_ref[0, 0, :, rows]
        grad_scores = exps * grad_probs
        value_sums[:, rows] += contract(grad_columns, exps, 1, 0)
        key_sums[:, rows] += contract(query_columns, grad_scores, 1, 0)
        keys = key_ref[0, rows, :]
        keys = jnp.where(lanes, keys, jnp.zeros_like(keys))
        grad_query = grad_query + contract(grad_scores, keys, 1, 0)
    grad_query_low = (grad_query * HD ** (-0.5)).astype(jnp.bfloat16)

    @pl.when(head == 0)
    def first_head():
        grad_query_ref[0] = grad_query_low

    @pl.when(head == 1)
    def second_head():
        grad_query_ref[0] = jnp.where(lanes, grad_query_low, grad_query_ref[0])

    @pl.when((step == pl.num_programs(1) - 1) & (head == 1))
    def write_sums():
        grad_key_ref[0] = (key_sums[...].T * HD ** (-0.5)).astype(jnp.bfloat16)
        grad_value_ref[0] = value_sums[...].T.astype(jnp.bfloat16)


def attend_back(exps, query_in, key_value, key_place, grad_mixed, mixed, inverse):
    units, query_total = mixed.shape[:2]
    key_total = key_value.shape[1]
    block_rows = min(1024, query_total)
    chunk = min(1024, key_total)
    query_spec = pl.BlockSpec((1, block_rows, PAIR), lambda unit, step, head: (unit, step, 0))
    whole_spec = pl.BlockSpec((1, key_total, PAIR), lambda unit, step, head: (unit, 0, 0))
    products = 8 * units * query_total * key_total * PAIR
    return pl.pallas_call(
        partial(attend_back_kernel, chunk),
        grid=(units, query_total // block_rows, 2),
        in_specs=[
            pl.BlockSpec(
                (1, 1, block_rows, key_total), lambda unit, step, head: (unit, head, step, 0)
            ),
            query_spec,
            pl.BlockSpec((1, key_total, PAIR), lambda unit, step, head: (unit, 0, key_place)),
            pl.BlockSpec((1, key_total, PAIR), lambda unit, step, head: (unit, 0, key_place + 1)),
            query_spec,
            query_spec,
            query_spec,
        ],
        out_specs=[query_spec, whole_spec, whole_spec],
        out_shape=[
            jax.ShapeDtypeStruct((units, query_total, PAIR), jnp.bfloat16),
            jax.ShapeDtypeStruct((units, key_total, PAIR), jnp.bfloat16),
            jax.ShapeDtypeStruct((units, key_total, PAIR), jnp.bfloat16),
        ],
        scratch_shapes=[pltpu.VMEM((PAIR, key_total), jnp.float32)] * 2,
        cost_estimate=pl.CostEstimate(
            flops=4 * products,
            bytes_accessed=4 * units * query_total * key_total,
            transcendentals=0,
        ),
        compiler_params=pltpu.CompilerParams(vmem_limit_bytes=62 << 20),
    )(exps, query_in, key_value, key_value, grad_mixed, mixed, inverse)


def swap_groups(array_in):
    dp_size = lax.axis_size("dp")
    tensor_size = lax.axis_size("tensor")
    pairs = [
        (row * tensor_size + column, column * dp_size + row)
        for row in range(dp_size)
        for column in range(tensor_size)
    ]
    return lax.ppermute(array_in, ("dp", "tensor"), pairs)


def spread_heads():
    return (D // PAIR) % (lax.axis_size("dp") * lax.axis_size("frame")) == 0


def to_heads(rows_in):
    tokens, pairs, columns = rows_in.shape
    axes = PLANE if spread_heads() else ("dp",)
    parts = math.prod(lax.axis_size(axis) for axis in axes)
    by_pair = jnp.transpose(rows_in, (1, 0, 2)).reshape(parts, pairs // parts, tokens, columns)
    moved = lax.all_to_all(by_pair, axes, 0, 0, tiled=True)
    return jnp.transpose(moved, (1, 0, 2, 3)).reshape(pairs // parts, parts * tokens, columns)


def to_tokens(units_in):
    axes = PLANE if spread_heads() else ("dp",)
    parts = math.prod(lax.axis_size(axis) for axis in axes)
    units, tokens_all, columns = units_in.shape
    by_place = jnp.transpose(
        units_in.reshape(units, parts, tokens_all // parts, columns), (1, 0, 2, 3)
    )
    moved = lax.all_to_all(by_place, axes, 0, 0, tiled=True)
    return jnp.transpose(
        moved.reshape(parts * units, tokens_all // parts, columns), (1, 0, 2)
    )


def gather_in(shard):
    tensor_size = lax.axis_size("tensor")
    whole = lax.all_gather(shard, EVERY, axis=0, tiled=True)
    return jnp.transpose(whole.reshape(tensor_size, D, -1), (1, 0, 2)).reshape(D, -1)


def gather_outs(shard):
    tensor_size = lax.axis_size("tensor")
    rows, columns = shard.shape
    whole = lax.all_gather(shard, EVERY, axis=0, tiled=True)
    return jnp.transpose(
        whole.reshape(tensor_size, D // columns, rows, columns), (0, 2, 1, 3)
    ).reshape(tensor_size * rows, D)


def scatter_in(grad_whole):
    tensor_size = lax.axis_size("tensor")
    stacked = jnp.transpose(
        to_half(grad_whole).reshape(D, tensor_size, -1), (1, 0, 2)
    ).reshape(tensor_size * D, -1)
    return lax.psum_scatter(stacked, EVERY, scatter_dimension=0, tiled=True).astype(jnp.float32)


def scatter_outs(grad_whole, columns):
    tensor_size = lax.axis_size("tensor")
    rows = grad_whole.shape[0] // tensor_size
    stacked = jnp.transpose(
        to_half(grad_whole).reshape(tensor_size, rows, D // columns, columns), (0, 2, 1, 3)
    ).reshape(-1, columns)
    return lax.psum_scatter(stacked, EVERY, scatter_dimension=0, tiled=True).astype(jnp.float32)


def swap_qkv(columns_in, outer, inner):
    rows = columns_in.shape[0]
    return jnp.transpose(
        columns_in.reshape(rows, outer, inner, PAIR), (0, 2, 1, 3)
    ).reshape(rows, outer * inner * PAIR)


def adam_update(master, first_old, second_old, grad_in, factor, fix_first, fix_second):
    clipped = grad_in * factor
    first_new = BETA_FIRST * first_old + (1.0 - BETA_FIRST) * clipped
    second_new = BETA_SECOND * second_old + (1.0 - BETA_SECOND) * clipped * clipped
    step_dir = first_new / fix_first / (jnp.sqrt(second_new / fix_second) + ADAM_EPS)
    master_new = master - LEARN_RATE * (step_dir + WEIGHT_DECAY * master)
    return (master_new, first_new, second_new)


def shards(
    latent,
    noise_draw,
    levels,
    context,
    step_count,
    w_in,
    w_outs,
    w_cond,
    w_time,
    w_patch,
    m_in,
    m_outs,
    m_cond,
    m_time,
    m_patch,
    v_in,
    v_outs,
    v_cond,
    v_time,
    v_patch,
):
    head_cols = D // lax.axis_size("tensor")
    pairs_block = head_cols // PAIR
    pairs_all = D // PAIR
    masters = (w_in, w_outs, w_cond, w_time, w_patch)
    clips, frames_here, patch_rows, width = latent.shape
    groups = clips * frames_here
    plane_index = lax.axis_index(PLANE)
    half_in, half_outs, half_cond, half_time, half_patch = [to_half(m) for m in masters]

    time_whole = lax.all_gather(half_time, PLANE, axis=0, tiled=True)
    levels_all = lax.all_gather(levels, PLANE, axis=0, tiled=False)
    fields = swap_groups(jnp.stack([latent, noise_draw]))
    patch_whole = lax.all_gather(half_patch, PLANE, axis=2, tiled=True)
    cond_whole = lax.all_gather(half_cond, PLANE, axis=0, tiled=True)
    w_qkv = gather_in(swap_qkv(half_in[:, : 3 * head_cols], 3, pairs_block))
    w_out = gather_outs(half_outs[:head_cols])
    w_up = gather_in(half_in[:, 3 * head_cols :])
    w_down = gather_outs(half_outs[head_cols:])
    w_first = time_whole[:TEMB]
    w_second = time_whole[TEMB:]
    w_embed = patch_whole[0]
    w_head = patch_whole[1]

    token_total = (TOKF * jnp.sum(FRAMES - context)).astype(jnp.float32)
    dp_size = lax.axis_size("dp")
    frame_size = lax.axis_size("frame")
    clip_ids = jnp.arange(dp_size * clips, dtype=jnp.int32).reshape(dp_size, 1, clips, 1)
    frame_ids = jnp.arange(FRAMES, dtype=jnp.int32).reshape(1, frame_size, 1, frames_here)
    clean_all = frame_ids < context[clip_ids]
    level_all = jnp.where(
        clean_all, 0, levels_all.reshape(dp_size, frame_size, clips, frames_here)
    ).astype(jnp.float32)
    embed_low = to_half(frequency_table(level_all.reshape(-1)))
    hidden_time = product(embed_low, w_first)
    first_low = to_half(jax.nn.silu(hidden_time))
    cond_vec = product(first_low, w_second)
    cond_low = to_half(jax.nn.silu(cond_vec))
    frame_index = lax.axis_index("frame")
    tensor_index = lax.axis_index("tensor")
    cond_frame = lax.dynamic_index_in_dim(
        cond_low.reshape(dp_size, frame_size, groups, D), frame_index, 1, keepdims=False
    )
    mod_blocks = product(cond_frame.reshape(dp_size * groups, D), cond_whole)
    mod_moved = lax.all_to_all(
        mod_blocks.reshape(dp_size, groups, -1), "tensor", 0, 0, tiled=True
    )
    modulation = jnp.transpose(mod_moved, (1, 0, 2)).reshape(groups, -1)
    pieces = [modulation[:, None, place * D : (place + 1) * D] for place in range(8)]

    def own_part(whole):
        part = lax.dynamic_index_in_dim(whole, tensor_index, 0, keepdims=False)
        return lax.dynamic_index_in_dim(part, frame_index, 0, keepdims=False)

    clean_frames = own_part(clean_all).reshape(groups)
    alpha_coef, sigma_coef = noise_terms(own_part(level_all))
    alpha_field = alpha_coef[:, :, None, None]
    sigma_field = sigma_coef[:, :, None, None]
    clean_field = fields[0].astype(jnp.float32)
    noise_field = fields[1].astype(jnp.float32)
    noisy_field = alpha_field * clean_field + sigma_field * noise_field
    target = alpha_field * noise_field - sigma_field * clean_field
    patch_low = to_half(patchify(noisy_field).reshape(groups, -1, PD))
    goal_rows = patchify(target).reshape(groups, -1, PD)
    rows_local = patch_low.shape[1]
    tokens = groups * rows_local

    residual_in = product(patch_low.reshape(-1, PD), w_embed).reshape(groups, rows_local, D)
    flat_one = to_half(modulate(residual_in, pieces[0], pieces[1])).reshape(tokens, D)
    qkv_rows = to_half(product(flat_one, w_qkv)).reshape(clips, -1, pairs_all, 3 * PAIR)
    spread = spread_heads()
    kept = []
    mixed_tokens = []
    for clip in range(clips):
        qkv_heads = to_heads(qkv_rows[clip])
        if spread:
            key_value, key_place = qkv_heads, 1
        else:
            key_value = lax.all_gather(qkv_heads[..., PAIR:], "frame", axis=1, tiled=True)
            key_place = 0
        exps, mixed_low, mixed, inverse = attend(qkv_heads, key_value, key_place)
        kept.append((exps, qkv_heads, key_value, key_place, mixed, inverse))
        mixed_tokens.append(to_tokens(mixed_low))
    mixed_flat = jnp.stack(mixed_tokens).reshape(tokens, D)
    attn_out = product(mixed_flat, w_out).reshape(groups, rows_local, D)
    residual_mid = residual_in + pieces[2] * attn_out
    flat_two = to_half(modulate(residual_mid, pieces[3], pieces[4])).reshape(tokens, D)
    hidden = product(flat_two, w_up)
    act_low = to_half(jax.nn.gelu(hidden, approximate=True))
    mlp_out = product(act_low, w_down).reshape(groups, rows_local, D)
    residual_out = residual_mid + pieces[5] * mlp_out
    final_low = to_half(modulate(residual_out, pieces[6], pieces[7])).reshape(tokens, D)
    predicted = cols_product(final_low, w_head).reshape(groups, rows_local, PD)
    weight_rows = (1.0 - clean_frames.astype(jnp.float32)).reshape(groups, 1, 1)
    error_rows = predicted - goal_rows
    loss_part = jnp.sum(weight_rows * error_rows * error_rows) / token_total

    grad_pred = to_half(2.0 * weight_rows * error_rows / token_total).reshape(tokens, PD)
    grad_head = rows_product(grad_pred, final_low)
    grad_final = product(grad_pred, w_head).reshape(groups, rows_local, D)
    grad_residual, grad_six, grad_seven = modulate_back(
        residual_out, pieces[6], pieces[7], grad_final
    )
    grad_five = jnp.sum(mlp_out * grad_residual, axis=1, keepdims=True)
    grad_mlp = to_half(pieces[5] * grad_residual).reshape(tokens, D)
    grad_down = rows_product(act_low, grad_mlp)
    final_down = scatter_outs(grad_down, half_outs.shape[1])
    grad_act = cols_product(grad_mlp, w_down)
    unused, gelu_back = jax.vjp(partial(jax.nn.gelu, approximate=True), hidden)
    grad_hidden = to_half(gelu_back(grad_act)[0])
    grad_up = rows_product(flat_two, grad_hidden)
    final_up = scatter_in(grad_up)
    grad_normed = cols_product(grad_hidden, w_up).reshape(groups, rows_local, D)
    grad_branch, grad_three, grad_four = modulate_back(
        residual_mid, pieces[3], pieces[4], grad_normed
    )
    grad_residual = grad_residual + grad_branch
    grad_two = jnp.sum(attn_out * grad_residual, axis=1, keepdims=True)
    grad_attn = to_half(pieces[2] * grad_residual).reshape(tokens, D)
    grad_mixed = to_half(cols_product(grad_attn, w_out)).reshape(clips, -1, pairs_all, PAIR)
    grad_out = rows_product(mixed_flat, grad_attn)
    final_out = scatter_outs(grad_out, half_outs.shape[1])
    grad_qkv_parts = []
    for clip in range(clips):
        exps, qkv_heads, key_value, key_place, mixed, inverse = kept[clip]
        grad_heads = to_heads(grad_mixed[clip])
        grad_query, grad_key, grad_value = attend_back(
            exps, qkv_heads, key_value, key_place, grad_heads, mixed, inverse
        )
        if not spread:
            grad_key, grad_value = [
                lax.psum_scatter(grad, "frame", scatter_dimension=1, tiled=True)
                for grad in (grad_key, grad_value)
            ]
        grad_qkv_parts.append(
            to_tokens(jnp.concatenate([grad_query, grad_key, grad_value], axis=-1))
        )
    grad_qkv = jnp.stack(grad_qkv_parts).reshape(tokens, 3 * D)
    grad_wqkv = rows_product(flat_one, grad_qkv)
    final_qkv = swap_qkv(scatter_in(grad_wqkv), pairs_block, 3)
    grad_normed = cols_product(grad_qkv, w_qkv).reshape(groups, rows_local, D)
    grad_branch, grad_zero, grad_one = modulate_back(residual_in, pieces[0], pieces[1], grad_normed)
    grad_residual = grad_residual + grad_branch
    grad_embed = rows_product(patch_low.reshape(-1, PD), to_half(grad_residual).reshape(-1, D))
    patch_sum = lax.psum(jnp.stack([grad_embed, grad_head]), EVERY)
    patch_cols = half_patch.shape[2]
    final_patch = lax.dynamic_slice_in_dim(patch_sum, plane_index * patch_cols, patch_cols, 2)
    grad_mod = jnp.concatenate(
        [grad_zero, grad_one, grad_two, grad_three, grad_four, grad_five, grad_six, grad_seven],
        axis=-1,
    )[:, 0, :]
    grad_mod_part = lax.psum_scatter(grad_mod, "dp", scatter_dimension=1, tiled=True)
    grad_mod_low = lax.all_gather(swap_groups(to_half(grad_mod_part)), PLANE, axis=0, tiled=True)
    cond_rows = half_cond.shape[0]
    cond_own = lax.dynamic_slice_in_dim(cond_low, plane_index * cond_rows, cond_rows, 1)
    final_cond = rows_product(cond_own, grad_mod_low)
    grad_cond_all = lax.psum(cols_product(grad_mod_low, cond_whole), "tensor")
    unused, silu_cond = jax.vjp(jax.nn.silu, cond_vec)
    grad_cond_low = to_half(silu_cond(grad_cond_all)[0])
    grad_second = rows_product(first_low, grad_cond_low)
    grad_first_act = cols_product(grad_cond_low, w_second)
    unused, silu_first = jax.vjp(jax.nn.silu, hidden_time)
    grad_hidden_time = to_half(silu_first(grad_first_act)[0])
    grad_first = rows_product(embed_low, grad_hidden_time)
    time_rows = half_time.shape[0]
    final_time = lax.dynamic_slice_in_dim(
        jnp.concatenate([grad_first, grad_second], axis=0), plane_index * time_rows, time_rows, 0
    )
    final_grads = (
        jnp.concatenate([final_qkv, final_up], axis=1),
        jnp.concatenate([final_out, final_down], axis=0),
        final_cond,
        final_time,
        final_patch,
    )
    split_square = sum((jnp.sum(grad_in * grad_in) for grad_in in final_grads[:3]))
    shared_square = sum(
        (jnp.sum(grad_in * grad_in) for grad_in in final_grads[3:])
    ) / lax.axis_size("tensor")
    totals = lax.psum((loss_part, split_square + shared_square), ("dp", "frame", "tensor"))
    loss_value = totals[0]
    grad_norm = jnp.sqrt(totals[1])
    factor = jnp.minimum(1.0, MAX_NORM / (grad_norm + 1e-06))
    steps_done = step_count[0].astype(jnp.float32)
    fix_first = 1.0 - BETA_FIRST**steps_done
    fix_second = 1.0 - BETA_SECOND**steps_done
    firsts = (m_in, m_outs, m_cond, m_time, m_patch)
    seconds = (v_in, v_outs, v_cond, v_time, v_patch)
    results = [
        adam_update(
            masters[which],
            firsts[which],
            seconds[which],
            final_grads[which],
            factor,
            fix_first,
            fix_second,
        )
        for which in range(5)
    ]
    return (
        loss_value,
        grad_norm,
        results[0][0],
        results[1][0],
        results[2][0],
        results[3][0],
        results[4][0],
        results[0][1],
        results[1][1],
        results[2][1],
        results[3][1],
        results[4][1],
        results[0][2],
        results[1][2],
        results[2][2],
        results[3][2],
        results[4][2],
        to_half(results[0][0]),
        to_half(results[1][0]),
        to_half(results[2][0]),
        to_half(results[3][0]),
        to_half(results[4][0]),
    )


def solution(mesh):
    placed = (
        P("dp", "frame", "tensor", None),
        P("dp", "frame", "tensor", None),
        P("dp", "frame"),
        P(),
        P(),
        P(("dp", "frame"), "tensor"),
        P("tensor", ("dp", "frame")),
        P(("dp", "frame"), "tensor"),
        P(("dp", "frame"), None),
        P(None, None, ("dp", "frame")),
        P(("dp", "frame"), "tensor"),
        P("tensor", ("dp", "frame")),
        P(("dp", "frame"), "tensor"),
        P(("dp", "frame"), None),
        P(None, None, ("dp", "frame")),
        P(("dp", "frame"), "tensor"),
        P("tensor", ("dp", "frame")),
        P(("dp", "frame"), "tensor"),
        P(("dp", "frame"), None),
        P(None, None, ("dp", "frame")),
    )
    return jax.shard_map(
        shards,
        mesh=mesh,
        in_specs=placed,
        out_specs=(
            P(),
            P(),
            P(("dp", "frame"), "tensor"),
            P("tensor", ("dp", "frame")),
            P(("dp", "frame"), "tensor"),
            P(("dp", "frame"), None),
            P(None, None, ("dp", "frame")),
            P(("dp", "frame"), "tensor"),
            P("tensor", ("dp", "frame")),
            P(("dp", "frame"), "tensor"),
            P(("dp", "frame"), None),
            P(None, None, ("dp", "frame")),
            P(("dp", "frame"), "tensor"),
            P("tensor", ("dp", "frame")),
            P(("dp", "frame"), "tensor"),
            P(("dp", "frame"), None),
            P(None, None, ("dp", "frame")),
            P(("dp", "frame"), "tensor"),
            P("tensor", ("dp", "frame")),
            P(("dp", "frame"), "tensor"),
            P(("dp", "frame"), None),
            P(None, None, ("dp", "frame")),
        ),
        check_vma=False,
    )
```

time: 3950 us -> 1980 us (0.50)
  matrix products: 1480 us -> 235 us
  waiting for transfers between devices: 1610 us -> 851 us
  other arithmetic: 491 us -> 89.8 us
  Pallas kernels: 0 us -> 340 us
  local copies, waits for them, and re-layouts: 206 us -> 273 us
  starting transfers between devices: 4.67 us -> 57.3 us
    dot_general x60 -> x0, matrix products: 838 us -> none  [the longest x12 310 us: one_block(): jnp.einsum('qhe,khe->hqk', grad_block, value_heads, preferred_element_typ...]
    all_gather x19 -> x6, waiting for transfers between devices: 767 us -> 58 us  [the longest x2 44.3 us: gather_in(): whole = lax.all_gather(shard, EVERY, axis=0, tiled=True)]
    pallas_call x0 -> x6, Pallas kernels: none -> 340 us  [the longest x3 207 us: attend_back(): pl.pallas_call(partial(attend_back_kernel, chunk), grid=(units, query_tot...]
    sub x24 -> x0, matrix products: 340 us -> none  [the longest x12 205 us: one_block(): soft_probs = jax.nn.softmax(scores, axis=-1)]
    convert_element_type x32 -> x15, other arithmetic: 362 us -> 29 us  [to_half(): return array_in.astype(jnp.bfloat16)]
    all_to_all x0 -> x13, waiting for transfers between devices: none -> 162 us  [the longest x6 121 us: to_heads(): moved = lax.all_to_all(by_pair, axes, 0, 0, tiled=True)]
    reduce_scatter x20 -> x5, waiting for transfers between devices: 765 us -> 609 us  [the longest x2 315 us: scatter_outs(): lax.psum_scatter(stacked, EVERY, scatter_dimension=0, tiled=True)]
    reshape x6 -> x14, local copies, waits for them, and re-layouts: 6.04 us -> 114 us  [the longest x2 33.7 us: gather_in(): whole.reshape(tensor_size, D, -1)]
  transfers between devices with their start and end apart: 43 -> 28, of which waited for: 30 -> 15; matrix products, arithmetic and copies ran while one was open for 53% -> 16% of each run, Pallas kernels for 0% -> 17%
where the time goes in v1:
time: 1980 us; the launch traced here: 1970 us
  waiting for transfers between devices  851 us (43%)
  Pallas kernels  340 us (17%)
  local copies, waits for them, and re-layouts  273 us (14%)
  matrix products  235 us (12%)
  blocking collectives  105 us (5%)
  other arithmetic  89.8 us (5%)
  starting transfers between devices  57.3 us (3%)
  between operations  22.9 us (1%)
    reduce_scatter x2, waiting for transfers between devices, scatter_outs(): lax.psum_scatter(stacked, EVERY, scatter_dimension=0, tiled=True)  315 us
    reduce_scatter x2, waiting for transfers between devices, scatter_in(): lax.psum_scatter(stacked, EVERY, scatter_dimension=0, tiled=True)  293 us
    pallas_call x3, Pallas kernels, attend_back(): pl.pallas_call(partial(attend_back_kernel, chunk), grid=(units, query_tot...  207 us
    pallas_call x3, Pallas kernels, attend(): pl.pallas_call(partial(attend_kernel, chunk), grid=(units, query_total //...  133 us
    all_to_all x6, waiting for transfers between devices, to_heads(): moved = lax.all_to_all(by_pair, axes, 0, 0, tiled=True)  121 us
    dot_general x6, matrix products, cols_product(): lax.dot_general(left_mat, right_mat, (((1,), (1,)), ((), ())), preferred_...  83.2 us
    dot_general x9, matrix products, product(): return jnp.dot(left_mat, right_mat, preferred_element_type=jnp.float32)  77.4 us
    dot_general x9, matrix products, rows_product(): lax.dot_general(left_mat, right_mat, (((0,), (0,)), ((), ())), preferred_...  74.9 us
  transfers between devices with their start and end apart: 28, of which 15 were waited for; matrix products, arithmetic and copies ran while one was open for 16% of the time, Pallas kernels for 17%

profile of v1, /device:TPU:0, one launch (start us, length us, event | category | flops | bytes accessed | tf_op | source)
XLA Modules:
  0.0 1973.5 jit_solution(6299559322798026334)
XLA Ops:
  18.9 22.0 %all-gather.1 = s32[8,3,8]{2,1,0:T(4,128)S(1)} all-gather(s32[1,3,8]{2,1,0:T(4,128)S(1)} %bitcast.341), channel_id=2, replica_groups=mesh['dp'=4,'frame'=2,'tensor'=4] {'dp','frame'}, dimensions={0}, use_global_device_ids=true | all-gather | bytes 864 | tf_op jit(solution)/shard_map/all_gather | solution.py:437
  41.1 16.2 all_gather.32
  98.1 19.7 all-to-all-done
  122.9 44.3 %all-gather.13.cloned.1.call-done = bf16[4096,768]{0,1:T(8,128)(2,1)} async-done(((bf16[128,768]{0,1:T(8,128)(2,1)}), bf16[4096,768]{0,1:T(8,128)(2,1)}) %all-gather.13.cloned.1.call-update) | async-done | bytes 6291472 | tf_op jit(solution)/shard_map/all_gather | solution.py:359
  203.2 36.4 %all-to-all-done.5 = bf16[8,1,512,384]{3,2,1,0:T(8,128)(2,1)} async-done(((bf16[8,1,512,384]{3,2,1,0:T(8,128)(2,1)}), bf16[8,1,512,384]{3,2,1,0:T(8,128)(2,1)}, u32[]{:S(2)}, u32[]{:S(2)}) %all-to-all-start.5) | async-done | bytes 3145760 | tf_op jit(solution)/shard_map/all_to_all | solution.py:340
  246.0 43.4 %all-to-all-done.3 = bf16[8,1,512,384]{3,2,1,0:T(8,128)(2,1)} async-done(((bf16[8,1,512,384]{3,2,1,0:T(8,128)(2,1)}), bf16[8,1,512,384]{3,2,1,0:T(8,128)(2,1)}, u32[]{:S(2)}, u32[]{:S(2)}) %all-to-all-start.3) | async-done | bytes 3145760 | tf_op jit(solution)/shard_map/all_to_all | solution.py:340
  293.8 44.1 %shard_map.364 = (bf16[1,2,4096,4096]{3,2,1,0:T(8,128)(2,1)}, bf16[1,4096,128]{2,1,0:T(8,128)(2,1)}, f32[1,4096,128]{2,1,0:T(8,128)}, f32[1,4096,128]{2,1,0:T(8,128)}) custom-call(bf16[1,4096,384]{2,1,0:T(8,128)(2,1)} %bitcast.31.query_ref.key_ref.value_ref, bf16[1,4096,384]{2,1,0:T(8,128)(2,1)} %bitcast.31.query_ref.key_ref.value_ref, ...), custom_call_target="tpu_custom_call" | custom-call | flops 34359738368 | bytes 67108864 | tf_op jit(solution)/shard_map/pallas_call | solution.py:186
  337.9 14.5 all-to-all-done.1
  356.0 44.3 %shard_map.363 = (bf16[1,2,4096,4096]{3,2,1,0:T(8,128)(2,1)}, bf16[1,4096,128]{2,1,0:T(8,128)(2,1)}, f32[1,4096,128]{2,1,0:T(8,128)}, f32[1,4096,128]{2,1,0:T(8,128)}) custom-call(bf16[1,4096,384]{2,1,0:T(8,128)(2,1)} %bitcast.23.query_ref.key_ref.value_ref, bf16[1,4096,384]{2,1,0:T(8,128)(2,1)} %bitcast.23.query_ref.key_ref.value_ref, ...), custom_call_target="tpu_custom_call" | custom-call | flops 34359738368 | bytes 67108864 | tf_op jit(solution)/shard_map/pallas_call | solution.py:186
  404.6 44.5 %shard_map.365 = (bf16[1,2,4096,4096]{3,2,1,0:T(8,128)(2,1)}, bf16[1,4096,128]{2,1,0:T(8,128)(2,1)}, f32[1,4096,128]{2,1,0:T(8,128)}, f32[1,4096,128]{2,1,0:T(8,128)}) custom-call(bf16[1,4096,384]{2,1,0:T(8,128)(2,1)} %bitcast.39.query_ref.key_ref.value_ref, bf16[1,4096,384]{2,1,0:T(8,128)(2,1)} %bitcast.39.query_ref.key_ref.value_ref, ...), custom_call_target="tpu_custom_call" | custom-call | flops 34359738368 | bytes 67108864 | tf_op jit(solution)/shard_map/pallas_call | solution.py:186
  490.7 14.9 reshape.475
  505.6 18.8 copy.133
  576.5 25.5 %multiply_convert_fusion = (bf16[1536,4096]{1,0:T(8,128)(2,1)}, f32[1536,4096]{1,0:T(8,128)}) fusion(bf16[1536,1024]{1,0:T(8,128)(2,1)S(1)} %bitcast.319, bf16[1024,4096]{1,0:T(8,128)(2,1)} %bitcast.302), kind=kOutput, calls=%fused_computation.10 | convolution fusion | flops 12941524992 | bytes 49283072 | tf_op jit(solution)/shard_map/dot_general | solution.py:42
  602.0 20.5 %fusion.82 = (f32[24,64]{1,0:T(8,128)S(1)}, f32[24,64,1024]{2,1,0:T(8,128)S(1)}, f32[24,64,1024]{2,1,0:T(8,128)}) fusion(f32[24,64,1024]{2,1,0:T(8,128)} %copy-done.3, f32[24,1024]{1,0:T(8,128)S(1)} %copy-done.47, bf16[24,64,4096]{2,1,0:T(8,128)(2,1)} %bitcast.342, bf16[4096,1024,1]{1,0,2:T(8,128)(2,1)} %reshape.528), kind=kOutput, calls=%fused_computation.199 | convolution fusion | flops 12889618432 | bytes 39950336 | tf_op jit(solution)/shard_map/dot_general | solution.py:42
  636.0 34.8 %fusion.6 = bf16[1536,4096]{1,0:T(8,128)(2,1)} fusion(f32[1536,4096]{1,0:T(8,128)} %get-tuple-element.140, bf16[1536,1024]{1,0:T(8,128)(2,1)S(1)} %bitcast.323, bf16[512,8,8,128]{3,2,1,0:T(8,128)(2,1)} %bitcast.287), kind=kOutput, calls=%fused_computation.9 | convolution fusion | flops 13010731008 | bytes 49283072 | tf_op jit(solution)/shard_map/dot_general | solution.py:52
  670.8 19.9 %multiply_reduce_fusion.6 = (f32[24,64]{1,0:T(8,128)S(1)}, f32[24,64,1024]{2,1,0:T(8,128)}) fusion(f32[24,64,1024]{2,1,0:T(8,128)S(1)} %bitcast.278, f32[24,1024]{1,0:T(8,128)S(1)} %copy-done.30, f32[24,64]{1,0:T(8,128)S(1)} %broadcast_multiply_fusion.1, bf16[24,64,4096]{2,1,0:T(8,128)(2,1)} %bitcast.343, bf16[1024,4096,1]{1,0,2:T(8,128)(2,1)} %reshape.530), kind=kOutput, calls=%fused_computation.31 | convolution fusion | flops 12891191296 | bytes 33665024 | tf_op jit(solution)/shard_map/dot_general | solution.py:52
  753.7 69.1 %shard_map.368 = (bf16[1,4096,128]{2,1,0:T(8,128)(2,1)}, bf16[1,4096,128]{2,1,0:T(8,128)(2,1)}, bf16[1,4096,128]{2,1,0:T(8,128)(2,1)}) custom-call(bf16[1,2,4096,4096]{3,2,1,0:T(8,128)(2,1)} %get-tuple-element.58.exps_ref, bf16[1,4096,384]{2,1,0:T(8,128)(2,1)} %bitcast.39.query_ref.key_ref.value_ref, ...), custom_call_target="tpu_custom_call" | custom-call | flops 68719476736 | bytes 67108864 | tf_op jit(solution)/shard_map/pallas_call | solution.py:290
  831.5 69.0 %shard_map.366 = (bf16[1,4096,128]{2,1,0:T(8,128)(2,1)}, bf16[1,4096,128]{2,1,0:T(8,128)(2,1)}, bf16[1,4096,128]{2,1,0:T(8,128)(2,1)}) custom-call(bf16[1,2,4096,4096]{3,2,1,0:T(8,128)(2,1)} %get-tuple-element.46.exps_ref, bf16[1,4096,384]{2,1,0:T(8,128)(2,1)} %bitcast.23.query_ref.key_ref.value_ref, ...), custom_call_target="tpu_custom_call" | custom-call | flops 68719476736 | bytes 67108864 | tf_op jit(solution)/shard_map/pallas_call | solution.py:290
  909.4 68.9 %shard_map.367 = (bf16[1,4096,128]{2,1,0:T(8,128)(2,1)}, bf16[1,4096,128]{2,1,0:T(8,128)(2,1)}, bf16[1,4096,128]{2,1,0:T(8,128)(2,1)}) custom-call(bf16[1,2,4096,4096]{3,2,1,0:T(8,128)(2,1)} %get-tuple-element.52.exps_ref, bf16[1,4096,384]{2,1,0:T(8,128)(2,1)} %bitcast.31.query_ref.key_ref.value_ref, ...), custom_call_target="tpu_custom_call" | custom-call | flops 68719476736 | bytes 67108864 | tf_op jit(solution)/shard_map/pallas_call | solution.py:290
  1008.8 15.0 all-to-all-done.10
  1044.8 15.1 dot_general.106
  1059.9 17.9 multiply_reduce_fusion
  1108.4 25.5 %all_gather.39 = bf16[192,2048]{1,0:T(8,128)(2,1)S(1)} all-gather(bf16[24,2048]{1,0:T(8,128)(2,1)S(1)} %collective-permute-done.1), channel_id=1, replica_groups=mesh['dp'=4,'frame'=2,'tensor'=4] {'dp','frame'}, dimensions={0}, use_global_device_ids=true | all-gather | bytes 884736 | tf_op jit(solution)/shard_map/all_gather | solution.py:578
  1165.9 18.5 convert_bitcast_fusion
  1211.2 18.5 convolution_convert_fusion.1
  1229.8 14.8 reshape.492
  1258.8 21.4 %all-reduce.4.cloned.1.call-done = f32[192,1024]{1,0:T(8,128)} async-done(((f32[192,1024]{1,0:T(8,128)}), f32[192,1024]{1,0:T(8,128)}) %all-reduce.4.cloned.1.call-update) | async-done | bytes 786448 | tf_op jit(solution)/shard_map/psum | solution.py:582
  1291.8 108.5 %reduce-scatter.6.cloned.1.call-done = bf16[128,768]{1,0:T(8,128)(2,1)} async-done(((bf16[4096,768]{1,0:T(8,128)(2,1)}), bf16[128,768]{1,0:T(8,128)(2,1)}) %reduce-scatter.6.cloned.1.call-update) | async-done | bytes 196624 | tf_op jit(solution)/shard_map/reduce_scatter | solution.py:377
  1405.5 133.9 %reduce-scatter.10.cloned.1.call-done = bf16[256,128]{1,0:T(8,128)(2,1)} async-done(((bf16[8192,128]{1,0:T(8,128)(2,1)}), bf16[256,128]{1,0:T(8,128)(2,1)}) %reduce-scatter.10.cloned.1.call-update) | async-done | bytes 65552 | tf_op jit(solution)/shard_map/reduce_scatter | solution.py:386
  1539.4 181.3 %reduce-scatter.12.cloned.1.call-done = bf16[1024,128]{1,0:T(8,128)(2,1)} async-done(((bf16[32768,128]{1,0:T(8,128)(2,1)}), bf16[1024,128]{1,0:T(8,128)(2,1)}) %reduce-scatter.12.cloned.1.call-update) | async-done | bytes 262160 | tf_op jit(solution)/shard_map/reduce_scatter | solution.py:386
  1722.4 184.8 %reduce-scatter.8.cloned.1.call-done = bf16[128,1024]{1,0:T(8,128)(2,1)} async-done(((bf16[4096,1024]{1,0:T(8,128)(2,1)}), bf16[128,1024]{1,0:T(8,128)(2,1)}) %reduce-scatter.8.cloned.1.call-update) | async-done | bytes 262160 | tf_op jit(solution)/shard_map/reduce_scatter | solution.py:377
  1911.0 40.9 %all-reduce = (f32[]{:T(128)}, f32[]{:T(128)}) all-reduce(f32[]{:T(128)S(6)} %div.156, f32[]{:T(128)S(6)} %add.312), channel_id=1, replica_groups=mesh['dp'=4,'frame'=2,'tensor'=4] {'dp','frame','tensor'}, use_global_device_ids=true, to_apply=%region_8.9 | all-reduce | flops 2 | bytes 16 | tf_op jit(solution)/shard_map/psum | solution.py:605
  (386 shorter events, 483.6 us)
Async XLA Ops:
  7.2 58.6 %all-gather.9.cloned.1.call-start = ((), (), s32[]{:S(2)}) async-start(), calls=%async_computation.18 | async-start | bytes 2949120 | tf_op jit(solution)/shard_map/all_gather | solution.py:436
  9.2 75.7 %all-gather.11.cloned.1.call-start = ((), (), s32[]{:S(2)}) async-start(), calls=%async_computation.19 | async-start | bytes 4718592 | tf_op jit(solution)/shard_map/all_gather | solution.py:440
  11.3 155.8 %all-gather.13.cloned.1.call-start = ((), (), s32[]{:S(2)}) async-start(), calls=%async_computation.20 | async-start | bytes 6488064 | tf_op jit(solution)/shard_map/all_gather | solution.py:359
  13.3 443.0 %all-gather.15.cloned.1.call-start = ((), (), s32[]{:S(2)}) async-start(), calls=%async_computation.21 | async-start | bytes 2162688 | tf_op jit(solution)/shard_map/all_gather | solution.py:366
  15.1 475.6 %all-gather.17.cloned.1.call-start = ((), (), s32[]{:S(2)}) async-start(), calls=%async_computation.22 | async-start | bytes 8650752 | tf_op jit(solution)/shard_map/all_gather | solution.py:359
  17.2 41.8 %collective-permute-start = (bf16[2,3,8,8,128]{4,3,2,1,0:T(8,128)(2,1)S(1)}, bf16[2,3,8,8,128]{4,3,2,1,0:T(8,128)(2,1)S(1)}, u32[]{:S(2)}, u32[]{:S(2)}) collective-permute-start(bf16[2,3,8,8,128]{4,3,2,1,0:T(8,128)(2,1)S(1)} %pad_maximum_fusion.8), channel_id=1, source_target_pairs={{0,0},{1,8},{2,16},{3,24},{8,1},{9,9},{10,17},{11,25},{16,2},{17,1... | collective-permute-start | bytes 294920 | tf_op jit(solution)/shard_map/ppermute | solution.py:328
  88.7 29.0 %all-to-all-start = ((f32[4,24,2048]{2,1,0:T(8,128)}), f32[4,24,2048]{2,1,0:T(8,128)S(1)}, u32[]{:S(2)}, u32[]{:S(2)}) async-start(f32[4,24,2048]{2,1,0:T(8,128)} %fusion.9), calls=%async_computation | async-start | bytes 1572864 | tf_op jit(solution)/shard_map/all_to_all | solution.py:470
  194.0 45.5 %all-to-all-start.5 = ((bf16[8,1,512,384]{3,2,1,0:T(8,128)(2,1)}), bf16[8,1,512,384]{3,2,1,0:T(8,128)(2,1)}, u32[]{:S(2)}, u32[]{:S(2)}) async-start(bf16[8,1,512,384]{3,2,1,0:T(8,128)(2,1)} %bitcast.296), calls=%async_computation.5 | async-start | bytes 6291456 | tf_op jit(solution)/shard_map/all_to_all | solution.py:340
  198.5 326.0 %all-gather.19.cloned.1.call-start = ((), (), s32[]{:S(2)}) async-start(), calls=%async_computation.23 | async-start | bytes 8650752 | tf_op jit(solution)/shard_map/all_gather | solution.py:366
  239.6 49.8 %all-to-all-start.3 = ((bf16[8,1,512,384]{3,2,1,0:T(8,128)(2,1)}), bf16[8,1,512,384]{3,2,1,0:T(8,128)(2,1)}, u32[]{:S(2)}, u32[]{:S(2)}) async-start(bf16[8,1,512,384]{3,2,1,0:T(8,128)(2,1)} %bitcast.299), calls=%async_computation.3 | async-start | bytes 6291456 | tf_op jit(solution)/shard_map/all_to_all | solution.py:340
  289.4 63.1 %all-to-all-start.1 = ((bf16[8,1,512,384]{3,2,1,0:T(8,128)(2,1)}), bf16[8,1,512,384]{3,2,1,0:T(8,128)(2,1)}, u32[]{:S(2)}, u32[]{:S(2)}) async-start(bf16[8,1,512,384]{3,2,1,0:T(8,128)(2,1)} %bitcast.298), calls=%async_computation.1 | async-start | bytes 6291456 | tf_op jit(solution)/shard_map/all_to_all | solution.py:340
  352.4 47.9 %all-to-all-start.4 = ((bf16[8,1,512,128]{3,2,1,0:T(8,128)(2,1)}), bf16[8,1,512,128]{3,2,1,0:T(8,128)(2,1)S(1)}, u32[]{:S(2)}, u32[]{:S(2)}) async-start(bf16[8,1,512,128]{3,2,1,0:T(8,128)(2,1)} %bitcast.330), calls=%async_computation.4 | async-start | bytes 2097152 | tf_op jit(solution)/shard_map/all_to_all | solution.py:351
  400.3 48.8 %all-to-all-start.2 = ((bf16[8,1,512,128]{3,2,1,0:T(8,128)(2,1)}), bf16[8,1,512,128]{3,2,1,0:T(8,128)(2,1)}, u32[]{:S(2)}, u32[]{:S(2)}) async-start(bf16[8,1,512,128]{3,2,1,0:T(8,128)(2,1)} %bitcast.331), calls=%async_computation.2 | async-start | bytes 2097152 | tf_op jit(solution)/shard_map/all_to_all | solution.py:351
  449.2 19.2 all-to-all-start.6
  454.8 171.0 %copy-start.87 = (f32[24]{0:T(128)}, f32[24]{0:T(128)S(1)}, u32[]{:S(2)}) copy-start(f32[24]{0:T(128)S(1)} %broadcast_multiply_fusion.3) | copy-start | bytes 292
  490.7 85.8 %copy-start.17 = (bf16[24,64,1024]{2,1,0:T(8,128)(2,1)}, bf16[24,64,1024]{2,1,0:T(8,128)(2,1)S(1)}, u32[]{:S(2)}) copy-start(bf16[24,64,1024]{2,1,0:T(8,128)(2,1)S(1)} %add_convert_fusion.2) | copy-start | bytes 9437188
  712.1 18.4 all-to-all-start.11
  730.6 18.4 all-to-all-start.7
  750.0 76.8 %all-to-all-start.9 = ((bf16[8,1,512,128]{3,2,1,0:T(8,128)(2,1)}), bf16[8,1,512,128]{3,2,1,0:T(8,128)(2,1)S(1)}, u32[]{:S(2)}, u32[]{:S(2)}) async-start(bf16[8,1,512,128]{3,2,1,0:T(8,128)(2,1)} %bitcast.69), calls=%async_computation.9 | async-start | bytes 2097152 | tf_op jit(solution)/shard_map/all_to_all | solution.py:340
  826.7 77.8 %all-to-all-start.12 = ((bf16[8,1,512,384]{3,2,1,0:T(8,128)(2,1)}), bf16[8,1,512,384]{3,2,1,0:T(8,128)(2,1)}, u32[]{:S(2)}, u32[]{:S(2)}) async-start(bf16[8,1,512,384]{3,2,1,0:T(8,128)(2,1)} %bitcast.81), calls=%async_computation.12 | async-start | bytes 6291456 | tf_op jit(solution)/shard_map/all_to_all | solution.py:351
  904.5 77.7 %all-to-all-start.8 = ((bf16[8,1,512,384]{3,2,1,0:T(8,128)(2,1)}), bf16[8,1,512,384]{3,2,1,0:T(8,128)(2,1)}, u32[]{:S(2)}, u32[]{:S(2)}) async-start(bf16[8,1,512,384]{3,2,1,0:T(8,128)(2,1)} %bitcast.63), calls=%async_computation.8 | async-start | bytes 6291456 | tf_op jit(solution)/shard_map/all_to_all | solution.py:351
  982.3 41.6 %all-to-all-start.10 = ((bf16[8,1,512,384]{3,2,1,0:T(8,128)(2,1)}), bf16[8,1,512,384]{3,2,1,0:T(8,128)(2,1)S(1)}, u32[]{:S(2)}, u32[]{:S(2)}) async-start(bf16[8,1,512,384]{3,2,1,0:T(8,128)(2,1)} %bitcast.297), calls=%async_computation.10 | async-start | bytes 6291456 | tf_op jit(solution)/shard_map/all_to_all | solution.py:351
  986.4 119.4 %reduce-scatter.14.cloned.1.call-start = ((), (), s32[]{:S(2)}) async-start(), calls=%async_computation.28 | async-start | bytes 983040 | tf_op jit(solution)/shard_map/reduce_scatter | solution.py:577
  1084.7 171.0 %all-reduce.6.cloned.1.call-start = ((), (), s32[]{:S(2)}) async-start(), calls=%async_computation.30 | async-start | bytes 262144 | tf_op jit(solution)/shard_map/psum | solution.py:570
  1106.9 1.4 collective-permute-start.1
  1108.3 172.0 %all-reduce.4.cloned.1.call-start = ((), (), s32[]{:S(2)}) async-start(), calls=%async_computation.29 | async-start | bytes 1572864 | tf_op jit(solution)/shard_map/psum | solution.py:582
  1139.4 261.0 %reduce-scatter.6.cloned.1.call-start = ((), (), s32[]{:S(2)}) async-start(), calls=%async_computation.24 | async-start | bytes 6488064 | tf_op jit(solution)/shard_map/reduce_scatter | solution.py:377
  1155.2 384.2 %reduce-scatter.10.cloned.1.call-start = ((), (), s32[]{:S(2)}) async-start(), calls=%async_computation.26 | async-start | bytes 2162688 | tf_op jit(solution)/shard_map/reduce_scatter | solution.py:386
  1165.2 555.4 %reduce-scatter.12.cloned.1.call-start = ((), (), s32[]{:S(2)}) async-start(), calls=%async_computation.27 | async-start | bytes 8650752 | tf_op jit(solution)/shard_map/reduce_scatter | solution.py:386
  1209.3 697.8 %reduce-scatter.8.cloned.1.call-start = ((), (), s32[]{:S(2)}) async-start(), calls=%async_computation.25 | async-start | bytes 8650752 | tf_op jit(solution)/shard_map/reduce_scatter | solution.py:377
  1284.8 667.9 %copy-start.25 = (f32[160,1024]{1,0:T(8,128)S(1)}, f32[160,1024]{1,0:T(8,128)}, u32[]{:S(2)}) copy-start(f32[160,1024]{1,0:T(8,128)} %param.28) | copy-start | bytes 1966084
  1288.5 667.4 %copy-start.13 = (f32[128,2048]{1,0:T(8,128)S(1)}, f32[128,2048]{1,0:T(8,128)}, u32[]{:S(2)}) copy-start(f32[128,2048]{1,0:T(8,128)} %param.27) | copy-start | bytes 3145732
  (91 other events, 1266.6 us)
Sparse Core Ops, SparseCore 0:
  10.5 35.0 all-gather.8
  48.1 36.7 all-gather.10
  88.3 78.8 all-gather.12
  170.0 66.8 all-gather.14
  240.2 129.9 all-gather.16
  373.6 78.7 all-gather.18
  1084.8 20.1 reduce-scatter.13
  1112.0 122.4 all-reduce.5
  1237.6 42.6 all-reduce.3
  1286.7 113.6 reduce-scatter.5
  1402.6 136.6 reduce-scatter.9
  1541.6 178.9 reduce-scatter.11
  1723.0 184.0 reduce-scatter.7
